TPU v7x, 128 devices: a whole 4x4x4 slice. The times are simulated.
128 devices in a mesh: row: 8 (over y, core), col: 16 (over z, x).
Axes of the slice: x: 4, y: 4, z: 4, core: 2. Of those that a mesh axis runs over, the one named last changes fastest.
Arguments:
- object_field: float32 [2, 2048, 4096], P(None, 'row', 'col'), may hold values from -0.4 to 0.4
- probe: float32 [2, 256, 256], replicated, may hold values from -8 to 8
- positions: int32 [2048, 2], P(('row', 'col')), may hold values from 0 to 3840, as said below
- amplitudes: bfloat16 [2048, 256, 256], P(('row', 'col')), may hold values from 0.25 to 2.5
- live: int32 [128], P(('row', 'col')), may hold values from 8 to 16, as said below
- kernel_first: float32 [2, 3, 3], replicated, may hold values from -4 to 4
- kernel_second: float32 [2, 3, 3], replicated, may hold values from -4 to 4
Outputs:
- object_out: float32 [2, 2048, 4096], P(None, 'row', 'col')
- probe_out: float32 [2, 256, 256], replicated
Inputs may be any that keep to these rules, and one draw needn't show every extreme that they name: `positions`: slot s is owned by device s // 16 of the row+col axis (row slowest); its window's top-left pixel lies in that device's tile (256 x 256), except that rows are clamped to at most 1792 and columns to at most 3840, so every window lies inside the object. `live`: some device uses all 16 slots; every device uses at least half of them.
All inputs are finite; a program needn't handle non-finite values.
Results may differ from a plain program's by a relative error of at most 0.006.
The roundings to bfloat16 on the way count: a program that leaves them out, or rounds other values in their place, can miss the bound.
Values sent between devices are 32-bit elements; how exact they have to be, the bound alone decides.
A program may use at most 128 MiB of HBM per device.

v0:
```python
import math

import jax
import jax.numpy as jnp
from jax import lax
from jax.sharding import PartitionSpec as P


def padded_2(block, sides, width):
    for axis, dim in sides:
        count = lax.axis_size(axis)
        forward = [(i, i + 1) for i in range(count - 1)]
        backward = [(target, source) for source, target in forward]
        low = lax.ppermute(
            lax.slice_in_dim(block, block.shape[dim] - width, None, axis=dim), axis, forward
        )
        high = lax.ppermute(lax.slice_in_dim(block, 0, width, axis=dim), axis, backward)
        block = jnp.concatenate([low, block, high], axis=dim)
    return block


def from_behind(block, axis, distance):
    devices = range(lax.axis_size(axis))
    route = [(i - distance, i) for i in devices if i - distance in devices]
    return lax.ppermute(block, axis, route)


def dft_tables(length):
    steps = jnp.arange(length, dtype=jnp.int32)
    product = steps[:, None] * steps[None, :] % length
    angle = product.astype(jnp.float32) * (2.0 * math.pi / length)
    scale = 1.0 / math.sqrt(length)
    return (
        (jnp.cos(angle) * scale).astype(jnp.bfloat16),
        (-jnp.sin(angle) * scale).astype(jnp.bfloat16),
    )


def matmul(left, right):
    return jnp.dot(left, right, preferred_element_type=jnp.float32)


def transform(table_re, table_im, value_re, value_im):
    half_re = (matmul(table_re, value_re) - matmul(table_im, value_im)).astype(jnp.bfloat16)
    half_im = (matmul(table_re, value_im) + matmul(table_im, value_re)).astype(jnp.bfloat16)
    out_re = matmul(half_re, table_re) - matmul(half_im, table_im)
    out_im = matmul(half_re, table_im) + matmul(half_im, table_re)
    return (out_re, out_im)


def position_terms(window, probe, amp, weight, table_re, table_im):
    exit_re = (probe[0] * window[0] - probe[1] * window[1]).astype(jnp.bfloat16)
    exit_im = (probe[0] * window[1] + probe[1] * window[0]).astype(jnp.bfloat16)
    spec_re, spec_im = transform(table_re, table_im, exit_re, exit_im)
    magnitude = jnp.sqrt(spec_re * spec_re + spec_im * spec_im)
    factor = amp.astype(jnp.float32) / jnp.maximum(magnitude, 0.25)
    diff_re = (factor * spec_re - spec_re).astype(jnp.bfloat16)
    diff_im = (factor * spec_im - spec_im).astype(jnp.bfloat16)
    change_re, change_im = transform(table_re, -table_im, diff_re, diff_im)
    change_re = change_re * weight
    change_im = change_im * weight
    object_term = jnp.stack(
        [probe[0] * change_re + probe[1] * change_im, probe[0] * change_im - probe[1] * change_re]
    )
    probe_term = jnp.stack(
        [
            window[0] * change_re + window[1] * change_im,
            window[0] * change_im - window[1] * change_re,
        ]
    )
    return (object_term, probe_term)


def correlate(field, kernel):
    padded = padded_2(field, (("row", 0), ("col", 1)), 1)
    rows, cols = field.shape
    total = jnp.zeros_like(field)
    for shift_a in range(3):
        for shift_b in range(3):
            total = (
                total
                + kernel[shift_a, shift_b]
                * padded[shift_a : shift_a + rows, shift_b : shift_b + cols]
            )
    return total


def body(object_field, probe, positions, amplitudes, live, kernel_first, kernel_second):
    tile_rows = object_field.shape[1]
    tile_cols = object_field.shape[2]
    width = probe.shape[1]
    slot_count = amplitudes.shape[0]
    col_count = lax.axis_size("col")
    total_slots = slot_count * lax.axis_size("row") * col_count
    table_re, table_im = dft_tables(width)
    base = jnp.stack([lax.axis_index("row") * tile_rows, lax.axis_index("col") * tile_cols])
    local = positions - base[None, :]
    slot_ids = jnp.arange(slot_count, dtype=jnp.int32)
    weights = (slot_ids < live[0]).astype(jnp.float32)
    zero = jnp.zeros((), jnp.int32)
    last_column = (lax.axis_index("col") == col_count - 1).astype(jnp.float32)
    batched_terms = jax.vmap(position_terms, in_axes=(0, None, 0, 0, None, None))
    for step in range(kernel_first.shape[0]):
        current = object_field
        current_probe = probe
        right = from_behind(current, "col", -1)
        wide = jnp.concatenate([current, right], axis=2)
        lower = from_behind(current, "row", -1)
        diagonal = from_behind(current, ("row", "col"), -(col_count + 1))
        diagonal = diagonal * (1.0 - last_column)
        below = jnp.concatenate([lower, diagonal], axis=2)
        extended = jnp.concatenate([wide, below], axis=1)

        def cut_window(offset):
            return lax.dynamic_slice(extended, (zero, offset[0], offset[1]), (2, width, width))

        windows = jax.vmap(cut_window)(local)
        object_terms, probe_terms = batched_terms(
            windows, current_probe, amplitudes, weights, table_re, table_im
        )
        probe_accum = jnp.sum(probe_terms, axis=0)

        def place(carry, item):
            offset, object_term = item
            start = (zero, offset[0], offset[1])
            placed = lax.dynamic_slice(carry, start, (2, width, width)) + object_term
            return (lax.dynamic_update_slice(carry, placed, start), None)

        accum, _ = lax.scan(place, jnp.zeros_like(extended), (local, object_terms))
        probe_total = lax.psum(probe_accum, ("row", "col"))
        spilled = from_behind(accum[:, :, tile_cols:], "col", 1)
        own = accum[:, :, :tile_cols]
        own = own.at[:, :, :width].add(spilled)
        dropped = from_behind(own[:, tile_rows:, :], "row", 1)
        gradient = own[:, :tile_rows, :].at[:, :width, :].add(dropped)
        stepped = current + gradient / slot_count
        probe = current_probe + 2.0 * probe_total / math.sqrt(total_slots)
        real_part = stepped[0] + jnp.tanh(correlate(stepped[1], kernel_first[step]))
        imag_part = stepped[1] + jnp.tanh(correlate(real_part, kernel_second[step]))
        object_field = jnp.stack([real_part, imag_part])
    return (object_field, probe)


def solution(mesh):
    return jax.shard_map(
        body,
        mesh=mesh,
        in_specs=(
            P(None, "row", "col"),
            P(),
            P(("row", "col"), None),
            P(("row", "col"), None, None),
            P(("row", "col")),
            P(),
            P(),
        ),
        out_specs=(P(None, "row", "col"), P()),
        check_vma=False,
    )
```

profile of v0, /device:TPU:1, one launch (start us, length us, event | category | flops | bytes accessed | tf_op | source)
XLA Modules:
  0.0 1193.4 jit_solution(6773229963341031082)
XLA Ops:
  15.8 9.7 collective-permute-done.2
  36.7 46.2 %while.32 = (s32[]{:T(128)}, f32[2,512,512]{2,1,0:T(8,128)S(1)}, s32[16,3]{0,1:T(4,128)S(1)}, f32[16,2,256,256]{3,2,0,1:T(8,128)}, s32[]{:T(128)}) while((s32[]{:T(128)}, f32[2,512,512]{2,1,0:T(8,128)S(1)}, s32[16,3]{0,1:T(4,128)S(1)}, f32[16,2,256,256]{3,2,0,1:T(8,128)}, s32[]{:T(128)}) %tuple.164), condition=%wide.while_cond.4, body=%wide.while_body.4.sunk | while | flops 2 | bytes 1050217 | solution.py:115
  132.1 227.3 %while.30 = (s32[]{:T(128)}, f32[2,512,512]{2,1,0:T(8,128)S(1)}, s32[16,2]{0,1:T(2,128)S(1)}, f32[16,2,256,256]{3,2,0,1:T(8,128)}, s32[]{:T(128)}, /*index=5*/s32[]{:T(128)}, s32[]{:T(128)}) while((s32[]{:T(128)}, f32[2,512,512]{2,1,0:T(8,128)S(1)}, s32[16,2]{0,1:T(2,128)S(1)}, f32[16,2,256,256]{3,2,0,1:T(8,128)}, s32[]{:T(128)}, ...), condition=%wide.region_1.2_spmd, body=%wide.region_0.1_spmd.sunk | while | flops 131080 | bytes 2621637 | solution.py:129
  164.9 9.9 dynamic_update_slice.8
  180.3 9.9 dynamic_update_slice.8
  209.1 10.2 dynamic_update_slice.8
  224.8 8.9 dynamic_update_slice.8
  280.5 10.4 dynamic_update_slice.8
  296.4 10.8 dynamic_update_slice.8
  366.4 14.2 %collective-permute-done.3 = f32[2,512,256]{2,1,0:T(8,128)S(1)} collective-permute-done((f32[2,512,256]{2,1,0:T(8,128)S(1)}, f32[2,512,256]{2,1,0:T(8,128)S(1)}, u32[]{:S(2)}, u32[]{:S(2)}) %collective-permute-start.3) | collective-permute-done | bytes 1048608 | tf_op jit(solution)/shard_map/ppermute | solution.py:25
  380.9 11.5 collective-permute-start.4
  457.0 159.5 %all-reduce.3.cloned.1.call-done = f32[2,256,256]{2,1,0:T(8,128)} async-done(((f32[2,256,256]{2,1,0:T(8,128)}), f32[2,256,256]{2,1,0:T(8,128)}) %all-reduce.3.cloned.1.call-update) | async-done | bytes 524304 | tf_op jit(solution)/shard_map/psum | solution.py:130
  625.0 46.8 %while.33 = (s32[]{:T(128)}, f32[2,512,512]{2,1,0:T(8,128)S(1)}, s32[16,3]{0,1:T(4,128)S(1)}, f32[16,2,256,256]{3,2,0,1:T(8,128)}, s32[]{:T(128)}) while((s32[]{:T(128)}, f32[2,512,512]{2,1,0:T(8,128)S(1)}, s32[16,3]{0,1:T(4,128)S(1)}, f32[16,2,256,256]{3,2,0,1:T(8,128)}, s32[]{:T(128)}) %tuple.180), condition=%wide.while_cond.5, body=%wide.while_body.5.sunk | while | flops 2 | bytes 1050217 | solution.py:115
  704.9 9.2 fusion.9
  722.0 234.1 %while.31 = (s32[]{:T(128)}, f32[2,512,512]{2,1,0:T(8,128)S(1)}, s32[16,2]{0,1:T(2,128)S(1)}, f32[16,2,256,256]{3,2,0,1:T(8,128)}, s32[]{:T(128)}, /*index=5*/s32[]{:T(128)}, s32[]{:T(128)}) while((s32[]{:T(128)}, f32[2,512,512]{2,1,0:T(8,128)S(1)}, s32[16,2]{0,1:T(2,128)S(1)}, f32[16,2,256,256]{3,2,0,1:T(8,128)}, s32[]{:T(128)}, ...), condition=%wide.region_5.6_spmd, body=%wide.region_4.5_spmd.sunk | while | flops 131080 | bytes 2621637 | solution.py:129
  756.0 9.9 dynamic_update_slice.9
  771.8 9.9 dynamic_update_slice.9
  801.5 10.2 dynamic_update_slice.9
  817.6 8.9 dynamic_update_slice.9
  860.4 8.8 dynamic_update_slice.9
  875.1 10.4 dynamic_update_slice.9
  891.4 10.8 dynamic_update_slice.9
  962.0 18.3 %collective-permute-done.16 = f32[2,512,256]{2,1,0:T(8,128)S(1)} collective-permute-done((f32[2,512,256]{2,1,0:T(8,128)S(1)}, f32[2,512,256]{2,1,0:T(8,128)S(1)}, u32[]{:S(2)}, u32[]{:S(2)}) %collective-permute-start.16) | collective-permute-done | bytes 1048608 | tf_op jit(solution)/shard_map/ppermute | solution.py:25
  1030.0 147.3 %all-reduce.5.cloned.1.call-done = f32[2,256,256]{2,1,0:T(8,128)} async-done(((f32[2,256,256]{2,1,0:T(8,128)}), f32[2,256,256]{2,1,0:T(8,128)}) %all-reduce.5.cloned.1.call-update) | async-done | bytes 524304 | tf_op jit(solution)/shard_map/psum | solution.py:130
  (400 shorter events, 557.0 us)
Async XLA Ops:
  7.2 609.4 %all-reduce.3.cloned.1.call-start = ((), (), s32[]{:S(2)}) async-start(), calls=%async_computation | async-start | bytes 1048576 | tf_op jit(solution)/shard_map/psum | solution.py:130
  7.2 18.2 %collective-permute-start.2 = (f32[2,256,256]{2,1,0:T(8,128)}, f32[2,256,256]{2,1,0:T(8,128)S(1)}, u32[]{:S(2)}, u32[]{:S(2)}) collective-permute-start(f32[2,256,256]{2,1,0:T(8,128)} %param.27), channel_id=1, source_target_pairs={{17,0},{18,1},{19,2},{20,3},{21,4},{22,5},{23,6},{24,7},{25,8},{26... | collective-permute-start | bytes 1572872 | tf_op jit(solution)/shard_map/ppermute | solution.py:25
  8.5 21.4 %collective-permute-start = (f32[2,256,256]{2,1,0:T(8,128)}, f32[2,256,256]{2,1,0:T(8,128)S(1)}, u32[]{:S(2)}, u32[]{:S(2)}) collective-permute-start(f32[2,256,256]{2,1,0:T(8,128)} %param.27), channel_id=1, source_target_pairs={{1,0},{2,1},{3,2},{4,3},{5,4},{6,5},{7,6},{8,7},{9,8},{10,9},{11,1... | collective-permute-start | bytes 1572872 | tf_op jit(solution)/shard_map/ppermute | solution.py:25
  9.8 20.9 %collective-permute-start.1 = (f32[2,256,256]{2,1,0:T(8,128)}, f32[2,256,256]{2,1,0:T(8,128)}, u32[]{:S(2)}, u32[]{:S(2)}) collective-permute-start(f32[2,256,256]{2,1,0:T(8,128)} %param.27), channel_id=1, source_target_pairs={{16,0},{32,16},{48,32},{64,48},{80,64},{96,80},{112,96},{17,1},{33... | collective-permute-start | bytes 1572872 | tf_op jit(solution)/shard_map/ppermute | solution.py:25
  359.5 21.1 %collective-permute-start.3 = (f32[2,512,256]{2,1,0:T(8,128)S(1)}, f32[2,512,256]{2,1,0:T(8,128)S(1)}, u32[]{:S(2)}, u32[]{:S(2)}) collective-permute-start(f32[2,512,256]{2,1,0:T(8,128)S(1)} %slice.505), channel_id=1, source_target_pairs={{0,1},{1,2},{2,3},{3,4},{4,5},{5,6},{6,7},{7,8},{8,9},{9,10},{10,1... | collective-permute-start | bytes 3145736 | tf_op jit(solution)/shard_map/ppermute | solution.py:25
  380.9 17.6 %collective-permute-start.4 = (f32[2,256,256]{2,1,0:T(8,128)S(1)}, f32[2,256,256]{2,1,0:T(8,128)S(1)}, u32[]{:S(2)}, u32[]{:S(2)}) collective-permute-start(f32[2,256,256]{2,1,0:T(8,128)S(1)} %slice.643), channel_id=1, source_target_pairs={{0,16},{16,32},{32,48},{48,64},{64,80},{80,96},{96,112},{1,17},{17... | collective-permute-start | bytes 1572872 | tf_op jit(solution)/shard_map/ppermute | solution.py:25
  398.6 6.4 collective-permute-start.5
  403.0 6.6 collective-permute-start.6
  409.7 6.1 collective-permute-start.7
  413.8 8.8 collective-permute-start.8
  428.7 6.4 collective-permute-start.10
  435.3 6.9 collective-permute-start.11
  439.4 7.0 collective-permute-start.12
  442.1 735.2 %all-reduce.5.cloned.1.call-start = ((), (), s32[]{:S(2)}) async-start(), calls=%async_computation.1 | async-start | bytes 1048576 | tf_op jit(solution)/shard_map/psum | solution.py:130
  452.5 165.3 %collective-permute-start.15 = (f32[2,256,256]{2,1,0:T(8,128)S(1)}, f32[2,256,256]{2,1,0:T(8,128)S(1)}, u32[]{:S(2)}, u32[]{:S(2)}) collective-permute-start(f32[2,256,256]{2,1,0:T(8,128)S(1)} %pad_maximum_fusion), channel_id=1, source_target_pairs={{17,0},{18,1},{19,2},{20,3},{21,4},{22,5},{23,6},{24,7},{25,8},{26... | collective-permute-start | bytes 1572872 | tf_op jit(solution)/shard_map/ppermute | solution.py:25
  453.8 164.0 %collective-permute-start.13 = (f32[2,256,256]{2,1,0:T(8,128)S(1)}, f32[2,256,256]{2,1,0:T(8,128)S(1)}, u32[]{:S(2)}, u32[]{:S(2)}) collective-permute-start(f32[2,256,256]{2,1,0:T(8,128)S(1)} %pad_maximum_fusion), channel_id=1, source_target_pairs={{1,0},{2,1},{3,2},{4,3},{5,4},{6,5},{7,6},{8,7},{9,8},{10,9},{11,1... | collective-permute-start | bytes 1572872 | tf_op jit(solution)/shard_map/ppermute | solution.py:25
  455.1 164.2 %collective-permute-start.14 = (f32[2,256,256]{2,1,0:T(8,128)S(1)}, f32[2,256,256]{2,1,0:T(8,128)}, u32[]{:S(2)}, u32[]{:S(2)}) collective-permute-start(f32[2,256,256]{2,1,0:T(8,128)S(1)} %pad_maximum_fusion), channel_id=1, source_target_pairs={{16,0},{32,16},{48,32},{64,48},{80,64},{96,80},{112,96},{17,1},{33... | collective-permute-start | bytes 1572872 | tf_op jit(solution)/shard_map/ppermute | solution.py:25
  956.2 24.0 %collective-permute-start.16 = (f32[2,512,256]{2,1,0:T(8,128)S(1)}, f32[2,512,256]{2,1,0:T(8,128)S(1)}, u32[]{:S(2)}, u32[]{:S(2)}) collective-permute-start(f32[2,512,256]{2,1,0:T(8,128)S(1)} %slice.561), channel_id=1, source_target_pairs={{0,1},{1,2},{2,3},{3,4},{4,5},{5,6},{6,7},{7,8},{8,9},{9,10},{10,1... | collective-permute-start | bytes 3145736 | tf_op jit(solution)/shard_map/ppermute | solution.py:25
  980.5 8.4 collective-permute-start.17
  989.1 6.4 collective-permute-start.18
  1003.0 6.9 collective-permute-start.21
  1016.1 7.8 collective-permute-start.22
  1025.6 153.6 %collective-permute-start.24 = (f32[258,1]{1,0:T(8,128)S(1)}, f32[258,1]{1,0:T(8,128)S(1)}, u32[]{:S(2)}, u32[]{:S(2)}) collective-permute-start(f32[258,1]{1,0:T(8,128)S(1)} %get-tuple-element.228), channel_id=1, source_target_pairs={{0,1},{1,2},{2,3},{3,4},{4,5},{5,6},{6,7},{7,8},{8,9},{9,10},{10,1... | collective-permute-start | bytes 3104 | tf_op jit(solution)/shard_map/ppermute | solution.py:14
  1028.7 150.5 %collective-permute-start.25 = (f32[258,1]{1,0:T(8,128)S(1)}, f32[258,1]{1,0:T(8,128)S(1)}, u32[]{:S(2)}, u32[]{:S(2)}) collective-permute-start(f32[258,1]{1,0:T(8,128)S(1)} %get-tuple-element.229), channel_id=1, source_target_pairs={{1,0},{2,1},{3,2},{4,3},{5,4},{6,5},{7,6},{8,7},{9,8},{10,9},{11,1... | collective-permute-start | bytes 3104 | tf_op jit(solution)/shard_map/ppermute | solution.py:17
  (24 other events, 962.9 us)
Sparse Core Ops, SparseCore 0:
  442.2 174.2 all-reduce.2
  1024.0 153.2 all-reduce.4
where the time goes:
time: 1210 us; the launch traced here: 1190 us
  local copies, waits for them, and re-layouts  409 us (34%)
  waiting for transfers between devices  390 us (32%)
  loops' own time  122 us (10%)
  other arithmetic  101 us (8%)
  starting transfers between devices  82.2 us (7%)
  matrix products  72.7 us (6%)
  between operations  16.1 us (1%)
    psum x2, waiting for transfers between devices, body(): probe_total = lax.psum(probe_accum, ('row', 'col'))  307 us
    dynamic_update_slice x32, local copies, waits for them, and re-layouts, place(): return (lax.dynamic_update_slice(carry, placed, start), None)  280 us
    another operation x2, loops' own time, body(): accum, _ = lax.scan(place, jnp.zeros_like(extended), (local, object_terms))  122 us
    gather x96, local copies, waits for them, and re-layouts  92.7 us
    dot_general x32, matrix products, matmul(): return jnp.dot(left, right, preferred_element_type=jnp.float32)  72.7 us
    ppermute x10, waiting for transfers between devices, from_behind(): return lax.ppermute(block, axis, route)  58.1 us
    add x32, other arithmetic, place(): placed = lax.dynamic_slice(carry, start, (2, width, width)) + object_term  40.4 us
    ppermute x10, starting transfers between devices, from_behind(): return lax.ppermute(block, axis, route)  36.8 us
  transfers between devices with their start and end apart: 28, of which 15 were waited for; matrix products, arithmetic and copies ran while one was open for 1% of the time, Pallas kernels for 0%

commit v1 on v0

v1 whole, which is shorter than its diff:
```python
import functools
import math

import jax
import jax.numpy as jnp
import ml_dtypes
import numpy as np
from jax import lax
from jax.experimental import pallas as pl
from jax.experimental.pallas import tpu as pltpu
from jax.sharding import PartitionSpec as P

W = 256
LANE = 128
ROWS = 8
COLS = 16
CHUNKS = 4
CH = W // CHUNKS
MESH = pl.DeviceIdType.MESH
F32 = jnp.float32
BF16 = jnp.bfloat16


def dft_tables():
    steps = np.arange(W)
    product = (steps[:, None] * steps[None, :]) % W
    angle = product.astype(np.float32) * np.float32(2.0 * math.pi / W)
    scale = np.float32(1.0 / math.sqrt(W))
    fr = (np.cos(angle) * scale).astype(ml_dtypes.bfloat16)
    fi = (-np.sin(angle) * scale).astype(ml_dtypes.bfloat16)
    left = np.block([[fr, -fi], [fi, fr]])
    return left, np.ascontiguousarray(left.T)


def dot(a, b):
    return jnp.dot(a, b, preferred_element_type=F32)


def window_kernel(pos, live, ext, probe, amps, left, right, acc, pacc, win, ebuf, dbuf, cbuf, amp_v, sems):
    slots = amps.shape[0]
    group = 2

    def amp_copy(s):
        return pltpu.make_async_copy(amps.at[s], amp_v.at[s], sems.at[s])

    for s in range(slots):
        amp_copy(s).start()

    def zero(i, _):
        rows = pl.ds(pl.multiple_of(i * 8, 8), 8)
        for part in range(2):
            for t in range(4):
                acc[part, t, rows, :] = jnp.zeros((8, LANE), F32)
        return 0

    lax.fori_loop(0, 64, zero, 0)

    def zero_probe(i, _):
        pacc[pl.ds(pl.multiple_of(i * 64, 64), 64), :] = jnp.zeros((64, LANE), F32)
        return 0

    lax.fori_loop(0, 16, zero_probe, 0)
    lane = lax.broadcasted_iota(jnp.int32, (32, LANE), 1)

    def place_of(s):
        r = pos[s, 0]
        c = pos[s, 1]
        q = c // LANE
        return r, q, c - q * LANE

    def step(p, _):
        for g in range(group):
            r, q, sh = place_of(p * group + g)

            def form(i, _):
                o = pl.multiple_of(i * 32, 32)
                rows = pl.ds(o, 32)
                keep = lane < LANE - sh
                w = []
                for part in range(2):
                    cuts = [pltpu.roll(ext[part, q + t, pl.ds(r + o, 32), :], LANE - sh, 1) for t in range(3)]
                    w.append([jnp.where(keep, cuts[t], cuts[t + 1]) for t in range(2)])
                for t in range(2):
                    cols = slice(t * LANE, (t + 1) * LANE)
                    win[g, 0, rows, cols] = w[0][t]
                    win[g, 1, rows, cols] = w[1][t]
                    pr = probe[pl.ds(t * W + o, 32), :]
                    pi = probe[pl.ds(2 * W + t * W + o, 32), :]
                    ebuf[g, rows, cols] = (pr * w[0][t] - pi * w[1][t]).astype(BF16)
                    ebuf[g, pl.ds(o + W, 32), cols] = (pr * w[1][t] + pi * w[0][t]).astype(BF16)
                return 0

            lax.fori_loop(0, 8, form, 0, unroll=True)
        for g in range(group):
            s = p * group + g
            half = dot(left[...], ebuf[g]).astype(BF16)
            spec = dot(jnp.concatenate([half[:W], half[W:]], axis=1), right[...])
            amp_copy(s).wait()
            amp = amp_v[s].astype(F32)
            sr, si = spec[:, :W], spec[:, W:]
            f = amp * lax.rsqrt(jnp.maximum(sr * sr + si * si, 0.0625)) - 1.0
            f = jnp.where(s < live[0], f, 0.0)
            dbuf[g, :W] = (f * sr).astype(BF16)
            dbuf[g, W:] = (f * si).astype(BF16)
        for g in range(group):
            back = dot(right[...], dbuf[g]).astype(BF16)
            cbuf[g] = dot(jnp.concatenate([back[:W], back[W:]], axis=1), left[...])
        for g in range(group):
            r, q, sh = place_of(p * group + g)

            def put(i, _):
                o = pl.multiple_of(i * 32, 32)
                rows = pl.ds(o, 32)
                keep = lane >= sh
                terms = [[], []]
                for t in range(2):
                    cols = slice(t * LANE, (t + 1) * LANE)
                    at_re = pl.ds(t * W + o, 32)
                    at_im = pl.ds(2 * W + t * W + o, 32)
                    pr = probe[at_re, :]
                    pi = probe[at_im, :]
                    cr = cbuf[g, rows, cols]
                    ci = cbuf[g, rows, W + t * LANE : W + (t + 1) * LANE]
                    wr = win[g, 0, rows, cols]
                    wi = win[g, 1, rows, cols]
                    pacc[at_re, :] += wr * cr + wi * ci
                    pacc[at_im, :] += wr * ci - wi * cr
                    terms[0].append(pltpu.roll(pr * cr + pi * ci, sh, 1))
                    terms[1].append(pltpu.roll(pr * ci - pi * cr, sh, 1))
                at = pl.ds(r + o, 32)
                for part in range(2):
                    a, b = terms[part]
                    acc[part, q, at, :] += jnp.where(keep, a, 0.0)
                    acc[part, q + 1, at, :] += jnp.where(keep, b, a)
                    acc[part, q + 2, at, :] += jnp.where(keep, 0.0, b)
                return 0

            lax.fori_loop(0, 8, put, 0, unroll=True)
        return 0

    lax.fori_loop(0, slots // group, step, 0)


VM = pl.BlockSpec(memory_space=pltpu.VMEM)
SM = pl.BlockSpec(memory_space=pltpu.SMEM)
ANY = pl.BlockSpec(memory_space=pl.ANY)
EXT = jax.ShapeDtypeStruct((2, 4, 2 * W, LANE), F32)
FLAT = jax.ShapeDtypeStruct((4 * W, LANE), F32)
TILE = jax.ShapeDtypeStruct((2, 2, W, LANE), F32)
DMA = pltpu.SemaphoreType.DMA


def window_call(local, live, ext, probe, amps, left, right):
    slots = amps.shape[0]
    group = 2
    return pl.pallas_call(
        window_kernel,
        out_shape=(EXT, FLAT),
        in_specs=[SM, SM, VM, VM, ANY, VM, VM],
        out_specs=(VM, VM),
        scratch_shapes=[
            pltpu.VMEM((group, 2, W, W), F32),
            pltpu.VMEM((group, 2 * W, W), BF16),
            pltpu.VMEM((group, 2 * W, W), BF16),
            pltpu.VMEM((group, W, 2 * W), F32),
            pltpu.VMEM((slots, W, W), BF16),
            DMA((slots,)),
        ],
        compiler_params=pltpu.CompilerParams(vmem_limit_bytes=48 * 2**20),
        name="windows",
    )(local, live, ext, probe, amps, left, right)


def remote(src, dst, send, recv, to):
    return pltpu.make_async_remote_copy(
        src_ref=src, dst_ref=dst, send_sem=send, recv_sem=recv, device_id=to, device_id_type=MESH
    )


def where_am_i():
    row = lax.axis_index("row")
    col = lax.axis_index("col")
    up = (lax.rem(row + ROWS - 1, ROWS), col)
    down = (lax.rem(row + 1, ROWS), col)
    west = (row, lax.rem(col + COLS - 1, COLS))
    east = (row, lax.rem(col + 1, COLS))
    return row, col, up, down, west, east


def greet(targets):
    barrier = pltpu.get_barrier_semaphore()
    for target in targets:
        pl.semaphore_signal(barrier, inc=1, device_id=target, device_id_type=MESH)
    pl.semaphore_wait(barrier, len(targets))


def chunk(k, base=0):
    return pl.ds(base + k * CH, CH)


def halo_start(ext, send, recv, west, up):
    own = slice(0, 2)
    far = slice(2, 4)
    to_west = [
        remote(ext.at[:, own, chunk(k), :], ext.at[:, far, chunk(k), :], send.at[k], recv.at[k], west)
        for k in range(CHUNKS)
    ]
    to_up = remote(
        ext.at[:, own, pl.ds(0, W), :], ext.at[:, own, pl.ds(W, W), :], send.at[CHUNKS], recv.at[CHUNKS], up
    )
    onward = [
        remote(
            ext.at[:, far, chunk(k), :],
            ext.at[:, far, chunk(k, W), :],
            send.at[CHUNKS + 1 + k],
            recv.at[CHUNKS + 1 + k],
            up,
        )
        for k in range(CHUNKS)
    ]
    for copy in to_west:
        copy.start()
    to_up.start()
    return to_west, to_up, onward


def halo_finish(copies):
    to_west, to_up, onward = copies
    for first, second in zip(to_west, onward):
        first.wait_recv()
        second.start()
    to_up.wait_recv()
    for copy in onward:
        copy.wait_recv()
    for copy in [*to_west, to_up, *onward]:
        copy.wait_send()


HALO_SEMS = 2 * CHUNKS + 1


def halo_kernel(obj, probe, ext, flat, send, recv):
    row, col, up, down, west, east = where_am_i()

    def lay(i, _):
        rows = pl.ds(pl.multiple_of(i * 32, 32), 32)
        for part in range(2):
            for t in range(2):
                ext[part, t, rows, :] = obj[part, rows, t * LANE : (t + 1) * LANE]
        return 0

    lax.fori_loop(0, W // 32, lay, 0)
    greet([up, down, west, east])
    copies = halo_start(ext, send, recv, west, up)

    def lay_probe(i, _):
        o = pl.multiple_of(i * 32, 32)
        for part in range(2):
            for t in range(2):
                flat[pl.ds((part * 2 + t) * W + o, 32), :] = probe[part, pl.ds(o, 32), t * LANE : (t + 1) * LANE]
        return 0

    lax.fori_loop(0, W // 32, lay_probe, 0)
    halo_finish(copies)


def halo_call(obj, probe):
    return pl.pallas_call(
        halo_kernel,
        out_shape=(EXT, FLAT),
        in_specs=[VM, VM],
        out_specs=(VM, VM),
        scratch_shapes=[DMA((HALO_SEMS,)), DMA((HALO_SEMS,))],
        compiler_params=pltpu.CompilerParams(
            collective_id=0, has_side_effects=True, vmem_limit_bytes=48 * 2**20
        ),
        name="first_halo",
    )(obj, probe)


TOP = 16
FRAME = W + 2 * TOP


def correlate_block(v, o, count, kernel, slabs, lane):
    sums = {}
    wanted = range(slabs[0] - 1, slabs[-1] + 2)
    for t in wanted:
        if t < 0 or t > 3:
            continue
        above, here, below = (v(t, o + a) for a in (-1, 0, 1))
        sums[t] = [above * kernel[0, b] + here * kernel[1, b] + below * kernel[2, b] for b in range(3)]
    out = []
    for t in slabs:
        before = pltpu.roll(sums[t][0], 1, 1)
        if t > 0:
            before = jnp.where(lane == 0, pltpu.roll(sums[t - 1][0], 1, 1), before)
        after = pltpu.roll(sums[t][2], LANE - 1, 1)
        if t < 3:
            after = jnp.where(lane == LANE - 1, pltpu.roll(sums[t + 1][2], LANE - 1, 1), after)
        out.append(sums[t][1] + before + after)
    return out


def update_kernel(
    last, acc, ext_old, pacc, flat_old, kf, ks, ext, flat,
    from_up, from_west, onward, rim_out, rim_in, frame, real,
    p1, h1, p2, h2, p3,
    y_send, y_recv, x_send, x_recv, rim_send, rim_recv, h_send, h_recv,
    a_send, a_recv, b_send, b_recv, c_send, c_recv, d_send, d_recv,
):
    row, col, up, down, west, east = where_am_i()
    core = lax.rem(row, 2)
    y = row // 2
    mate = (row + 1 - 2 * core, col)
    beyond = (lax.rem(row + ROWS - 1 + 2 * core, ROWS), col)
    in_y = [(lax.rem(row + 2 * d, ROWS), col) for d in range(1, 4)]
    in_col = [(row, lax.rem(col + d, COLS)) for d in range(1, COLS)]
    greet([mate, beyond, *in_y, *in_col])

    y_copies = [
        remote(acc.at[:, pl.ds(2, 2), chunk(k, W), :], from_up.at[:, pl.ds(2, 2), chunk(k), :], y_send.at[k], y_recv.at[k], down)
        for k in range(CHUNKS)
    ]
    y_copies.append(
        remote(acc.at[:, pl.ds(0, 2), pl.ds(W, W), :], from_up.at[:, pl.ds(0, 2), :, :], y_send.at[CHUNKS], y_recv.at[CHUNKS], down)
    )
    for copy in y_copies:
        copy.start()

    mine = pl.multiple_of(core * 512, 512)
    other = pl.multiple_of(512 - core * 512, 512)
    a_copies = [remote(pacc.at[pl.ds(other, 512), :], p1, a_send.at[0], a_recv.at[0], mate)]
    a_copies[0].start()

    x_copies = []
    for k in range(CHUNKS):
        y_copies[k].wait_recv()

        def join(i, _):
            o = pl.multiple_of(i * 16, 16)
            for part in range(2):
                for t in range(2):
                    onward[part, t, pl.ds(k * CH + o, 16), :] = (
                        acc[part, 2 + t, pl.ds(k * CH + o, 16), :] + from_up[part, 2 + t, pl.ds(k * CH + o, 16), :]
                    )
            return 0

        lax.fori_loop(0, CH // 16, join, 0)
        copy = remote(onward.at[:, :, chunk(k), :], from_west.at[:, :, chunk(k), :], x_send.at[k], x_recv.at[k], east)
        copy.start()
        x_copies.append(copy)

    a_copies[0].wait_recv()

    def join_half(i, _):
        o = pl.multiple_of(i * 64, 64)
        h1[pl.ds(o, 64), :] = pacc[pl.ds(mine + o, 64), :] + p1[pl.ds(o, 64), :]
        return 0

    lax.fori_loop(0, 8, join_half, 0)
    b_copies = []
    for d in range(1, 4):
        block = pl.multiple_of(lax.rem(y + d, 4) * LANE, LANE)
        b_copies.append(remote(h1.at[pl.ds(block, LANE), :], p2.at[d - 1], b_send.at[d - 1], b_recv.at[d - 1], in_y[d - 1]))
    for copy in b_copies:
        copy.start()

    for t in range(4):
        for part in range(2):
            frame[part, t, pl.ds(0, 8), :] = jnp.zeros((8, LANE), F32)
            frame[part, t, pl.ds(FRAME - 8, 8), :] = jnp.zeros((8, LANE), F32)

    def step_rows(k):
        def add(i, _):
            o = pl.multiple_of(k * CH + i * 16, 16)
            rows = pl.ds(o, 16)
            for part in range(2):
                for t in range(2):
                    total = acc[part, t, rows, :] + from_up[part, t, rows, :] + from_west[part, t, rows, :]
                    frame[part, 1 + t, pl.ds(TOP + o, 16), :] = ext_old[part, t, rows, :] + total * (1.0 / 16.0)
            return 0

        lax.fori_loop(0, CH // 16, add, 0)

    y_copies[CHUNKS].wait_recv()
    for k in range(CHUNKS // 2):
        x_copies[k].wait_recv()
        step_rows(k)

    for copy in b_copies:
        copy.wait_recv()
    here = pl.multiple_of(y * LANE, LANE)
    h2[...] = h1[pl.ds(here, LANE), :] + p2[0] + p2[1] + p2[2]
    c_copies = []
    for d in range(1, COLS):
        block = pl.multiple_of(lax.rem(col + d, COLS) * 8, 8)
        c_copies.append(remote(h2.at[pl.ds(block, 8), :], p3.at[d], c_send.at[d], c_recv.at[d], in_col[d - 1]))
    for copy in c_copies:
        copy.start()

    for k in range(CHUNKS // 2, CHUNKS):
        x_copies[k].wait_recv()
        step_rows(k)

    for part in range(2):
        rim_out[0, part, :, :] = frame[part, 1, pl.ds(TOP, W), :].T[:8, :]
        rim_out[1, part, :, :] = frame[part, 2, pl.ds(TOP, W), :].T[LANE - 8 :, :]
    rims = [
        remote(rim_out.at[0], rim_in.at[0], rim_send.at[0], rim_recv.at[0], west),
        remote(rim_out.at[1], rim_in.at[1], rim_send.at[1], rim_recv.at[1], east),
    ]
    rims[0].start()
    rims[1].start()

    for copy in c_copies:
        copy.wait_recv()
    own = pl.multiple_of(col * 8, 8)
    total = h2[pl.ds(own, 8), :]
    for d in range(1, COLS):
        total = total + p3[d]
    piece = pl.multiple_of(core * 512 + y * LANE + col * 8, 8)
    flat[pl.ds(piece, 8), :] = flat_old[pl.ds(piece, 8), :] + total * (2.0 / math.sqrt(2048.0))
    d_copies = []
    for d in range(1, COLS):
        d_copies.append(
            remote(flat.at[pl.ds(piece, 8), :], flat.at[pl.ds(piece, 8), :], d_send.at[d], d_recv.at[d], in_col[d - 1])
        )
    for copy in d_copies:
        copy.start()

    rims[0].wait_recv()
    rims[1].wait_recv()
    blank = jnp.zeros((LANE - 8, W), F32)
    for part in range(2):
        right_rim = jnp.where(col < COLS - 1, rim_in[0, part, :, :], 0.0)
        left_rim = jnp.where(col > 0, rim_in[1, part, :, :], 0.0)
        frame[part, 3, pl.ds(TOP, W), :] = jnp.concatenate([right_rim, blank], axis=0).T
        frame[part, 0, pl.ds(TOP, W), :] = jnp.concatenate([blank, left_rim], axis=0).T
    rows_out = [
        remote(frame.at[:, :, pl.ds(TOP, 8), :], frame.at[:, :, pl.ds(TOP + W, 8), :], rim_send.at[2], rim_recv.at[2], up),
        remote(frame.at[:, :, pl.ds(TOP + W - 8, 8), :], frame.at[:, :, pl.ds(TOP - 8, 8), :], rim_send.at[3], rim_recv.at[3], down),
    ]
    rows_out[0].start()
    rows_out[1].start()

    def gathered(first, count, send, recv, to):
        return remote(flat.at[pl.ds(first, count), :], flat.at[pl.ds(first, count), :], send, recv, to)

    for copy in d_copies:
        copy.wait_recv()
    quarter = pl.multiple_of(core * 512 + y * LANE, LANE)
    for d in range(1, 4):
        b_copies.append(gathered(quarter, LANE, b_send.at[2 + d], b_recv.at[2 + d], in_y[d - 1]))
        b_copies[-1].start()

    rows_out[0].wait_recv()
    rows_out[1].wait_recv()
    for part in range(2):
        for t in range(4):
            top = pl.ds(TOP - 8, 8)
            low = pl.ds(TOP + W, 8)
            frame[part, t, top, :] = jnp.where(row > 0, frame[part, t, top, :], 0.0)
            frame[part, t, low, :] = jnp.where(row < ROWS - 1, frame[part, t, low, :], 0.0)

    lane8 = lax.broadcasted_iota(jnp.int32, (8, LANE), 1)
    lane16 = lax.broadcasted_iota(jnp.int32, (16, LANE), 1)
    west_on = (col > 0).astype(F32)
    east_on = (col < COLS - 1).astype(F32)

    def first(i, _):
        o = pl.multiple_of(8 + i * 8, 8)
        parts = correlate_block(lambda t, at: frame[1, t, pl.ds(at, 8), :], o, 8, kf, range(4), lane8)
        keep_row = jnp.where(i == 0, (row > 0).astype(F32), jnp.where(i == 33, (row < ROWS - 1).astype(F32), 1.0))
        for t in range(4):
            value = frame[0, t, pl.ds(o, 8), :] + jnp.tanh(parts[t])
            keep = keep_row
            if t == 0:
                keep = keep * west_on
            if t == 3:
                keep = keep * east_on
            real[t, pl.ds(o, 8), :] = value * keep
        return 0

    lax.fori_loop(0, 34, first, 0)

    def second(i, _):
        o = pl.multiple_of(TOP + i * 16, 16)
        at = pl.ds(pl.multiple_of(i * 16, 16), 16)
        parts = correlate_block(lambda t, a: real[t, pl.ds(a, 16), :], o, 16, ks, range(1, 3), lane16)
        for t in range(2):
            ext[0, t, at, :] = real[1 + t, pl.ds(o, 16), :]
            ext[1, t, at, :] = frame[1, 1 + t, pl.ds(o, 16), :] + jnp.tanh(parts[t])
        return 0

    lax.fori_loop(0, 16, second, 0)

    if not last:
        copies = halo_start(ext, h_send, h_recv, west, up)

    for copy in b_copies[3:]:
        copy.wait_recv()
    a_copies.append(gathered(mine, 512, a_send.at[1], a_recv.at[1], mate))
    a_copies[1].start()
    if not last:
        halo_finish(copies)
    a_copies[1].wait_recv()
    for copy in [*y_copies, *x_copies, *a_copies, *b_copies, *c_copies, *d_copies, *rims, *rows_out]:
        copy.wait_send()


def update_call(last, acc, ext, pacc, flat, kf, ks):
    return pl.pallas_call(
        functools.partial(update_kernel, last),
        out_shape=(TILE if last else EXT, FLAT),
        in_specs=[VM, VM, VM, VM, SM, SM],
        out_specs=(VM, VM),
        scratch_shapes=[
            pltpu.VMEM((2, 4, W, LANE), F32),
            pltpu.VMEM((2, 2, W, LANE), F32),
            pltpu.VMEM((2, 2, W, LANE), F32),
            pltpu.VMEM((2, 2, 8, W), F32),
            pltpu.VMEM((2, 2, 8, W), F32),
            pltpu.VMEM((2, 4, FRAME, LANE), F32),
            pltpu.VMEM((4, FRAME, LANE), F32),
            pltpu.VMEM((512, LANE), F32),
            pltpu.VMEM((512, LANE), F32),
            pltpu.VMEM((3, LANE, LANE), F32),
            pltpu.VMEM((LANE, LANE), F32),
            pltpu.VMEM((COLS, 8, LANE), F32),
            DMA((CHUNKS + 1,)), DMA((CHUNKS + 1,)),
            DMA((CHUNKS,)), DMA((CHUNKS,)),
            DMA((4,)), DMA((4,)),
            DMA((HALO_SEMS,)), DMA((HALO_SEMS,)),
            DMA((2,)), DMA((2,)),
            DMA((6,)), DMA((6,)),
            DMA((COLS,)), DMA((COLS,)),
            DMA((COLS,)), DMA((COLS,)),
        ],
        compiler_params=pltpu.CompilerParams(
            collective_id=2 if last else 1, has_side_effects=True, vmem_limit_bytes=48 * 2**20
        ),
        name="last_update" if last else "update",
    )(acc, ext, pacc, flat, kf, ks)


def body(object_field, probe, positions, amplitudes, live, kernel_first, kernel_second):
    left, right = dft_tables()
    left, right = jnp.asarray(left), jnp.asarray(right)
    base = jnp.stack([lax.axis_index("row") * W, lax.axis_index("col") * W])
    local = positions - base[None, :]
    iters = kernel_first.shape[0]
    ext, flat = halo_call(object_field, probe)
    for step in range(iters):
        acc, pacc = window_call(local, live, ext, flat, amplitudes, left, right)
        ext, flat = update_call(step == iters - 1, acc, ext, pacc, flat, kernel_first[step], kernel_second[step])

    def whole(x):
        return x.reshape(2, 2, W, LANE).transpose(0, 2, 1, 3).reshape(2, W, W)

    return whole(ext), whole(flat)


def solution(mesh):
    return jax.shard_map(
        body,
        mesh=mesh,
        in_specs=(
            P(None, "row", "col"),
            P(),
            P(("row", "col"), None),
            P(("row", "col"), None, None),
            P(("row", "col")),
            P(),
            P(),
        ),
        out_specs=(P(None, "row", "col"), P()),
        check_vma=False,
    )
```

time: 1210 us -> 185 us (0.15); the launches traced: 1190 us -> 184 us
  local copies, waits for them, and re-layouts: 409 us -> 11.1 us
  waiting for transfers between devices: 390 us -> 0 us
  Pallas kernels: 0 us -> 172 us
  loops' own time: 122 us -> 0 us
  other arithmetic: 101 us -> 0.08 us
  starting transfers between devices: 82.2 us -> 0 us
  matrix products: 72.7 us -> 0 us
  between operations: 16.1 us -> 1.37 us
    psum x2 -> x0, waiting for transfers between devices: 307 us -> none  [body(): probe_total = lax.psum(probe_accum, ('row', 'col'))]
    dynamic_update_slice x32 -> x0, local copies, waits for them, and re-layouts: 280 us -> none  [place(): return (lax.dynamic_update_slice(carry, placed, start), None)]
    pallas_call x0 -> x5, Pallas kernels: none -> 172 us  [the longest x2 95.8 us: update_call(): pl.pallas_call(functools.partial(update_kernel, last), out_shape=(TILE if...]
    another operation x4 -> x0, loops' own time: 122 us -> none  [the longest x2 122 us: body(): accum, _ = lax.scan(place, jnp.zeros_like(extended), (local, object_terms))]
    gather x96 -> x0, local copies, waits for them, and re-layouts: 92.7 us -> none
    ppermute x26 -> x0, waiting for transfers between devices: 83.6 us -> none  [the longest x10 58.1 us: from_behind(): return lax.ppermute(block, axis, route)]
    ppermute x26 -> x0, starting transfers between devices: 82.1 us -> none  [the longest x10 36.8 us: from_behind(): return lax.ppermute(block, axis, route)]
    dot_general x32 -> x0, matrix products: 72.7 us -> none  [matmul(): return jnp.dot(left, right, preferred_element_type=jnp.float32)]
  transfers between devices with their start and end apart: 28 -> 0, of which waited for: 15 -> 0; matrix products, arithmetic and copies ran while one was open for 1% -> 0% of each run, Pallas kernels for 0% -> 0%
where the time goes in v1:
time: 185 us; the launch traced here: 184 us
  Pallas kernels  172 us (93%)
  local copies, waits for them, and re-layouts  11.1 us (6%)
    pallas_call x2, Pallas kernels, update_call(): pl.pallas_call(functools.partial(update_kernel, last), out_shape=(TILE if...  95.8 us
    pallas_call x2, Pallas kernels, window_call(): pl.pallas_call(window_kernel, out_shape=(EXT, FLAT), in_specs=[SM, SM, VM...  54.3 us
    pallas_call x1, Pallas kernels, halo_call(): pl.pallas_call(halo_kernel, out_shape=(EXT, FLAT), in_specs=[VM, VM], out...  21.6 us
    unnamed x20, local copies, waits for them, and re-layouts  8.58 us

profile of v1, /device:TPU:1, one launch (start us, length us, event | category | flops | bytes accessed | tf_op | source)
XLA Modules:
  0.0 184.3 jit_solution(17080282569368214045)
XLA Ops:
  1.3 0.1 pad_add_fusion
  1.4 0.8 fusion.1
  2.1 0.8 fusion
  2.9 0.8 copy.13
  3.7 1.0 copy-done.6
  4.7 1.0 copy-done.7
  5.7 21.6 %first_halo.1 = (f32[2,4,512,128]{3,2,1,0:T(8,128)S(1)}, f32[1024,128]{1,0:T(8,128)S(1)}) custom-call(f32[2,256,256]{2,1,0:T(8,128)S(1)} %copy-done.6, f32[2,256,256]{2,1,0:T(8,128)S(1)} %copy-done.7), custom_call_target="tpu_custom_call" | custom-call | tf_op jit(solution)/shard_map/first_halo/pallas_call | solution.py:268
  27.4 0.0 copy-start.1
  27.4 1.3 copy-done.1
  28.7 1.0 copy-done.2
  29.8 1.0 copy-done.4
  30.8 27.0 %windows.2 = (f32[2,4,512,128]{3,2,1,0:T(8,128)S(1)}, f32[1024,128]{1,0:T(8,128)S(1)}) custom-call(s32[16,2]{1,0:T(8,128)S(1)} %broadcast_subtract_fusion.pos, s32[1]{0:T(128)S(6)} %copy.28.live, f32[2,4,512,128]{3,2,1,0:T(8,128)} %copy-done.1, f32[1024,128]{1,0:T(8,128)S(1)} %get-tuple-element.13.probe.flat_old, bf16[16,256,256]{2,1,0:T(8,128)(2,1)} %amps.3, ...), custom_call_target="tpu_custom_call" | custom-call | tf_op jit(solution)/shard_map/windows/pallas_call | solution.py:156
  57.8 0.0 copy-start.3
  57.8 0.0 copy-start.5
  57.8 54.0 %update.1 = (f32[2,4,512,128]{3,2,1,0:T(8,128)S(1)}, f32[1024,128]{1,0:T(8,128)S(1)}) custom-call(f32[2,4,512,128]{3,2,1,0:T(8,128)S(1)} %get-tuple-element.14.acc, f32[2,4,512,128]{3,2,1,0:T(8,128)} %copy-done.1, f32[1024,128]{1,0:T(8,128)S(1)} %get-tuple-element.15.pacc, f32[1024,128]{1,0:T(8,128)S(1)} %get-tuple-element.13.probe.flat_old, ...), custom_call_target="tpu_custom_call" | custom-call | tf_op jit(solution)/shard_map/update/pallas_call | solution.py:513
  111.8 0.0 copy-start
  111.9 1.3 copy-done
  113.2 0.0 copy-done.3
  113.2 0.0 copy-done.5
  113.2 27.3 %windows.3 = (f32[2,4,512,128]{3,2,1,0:T(8,128)S(1)}, f32[1024,128]{1,0:T(8,128)S(1)}) custom-call(s32[16,2]{1,0:T(8,128)S(1)} %broadcast_subtract_fusion.pos, s32[1]{0:T(128)S(6)} %copy.28.live, f32[2,4,512,128]{3,2,1,0:T(8,128)} %copy-done, f32[1024,128]{1,0:T(8,128)S(1)} %get-tuple-element.17.probe.flat_old, bf16[16,256,256]{2,1,0:T(8,128)(2,1)} %amps.3, ...), custom_call_target="tpu_custom_call" | custom-call | tf_op jit(solution)/shard_map/windows/pallas_call | solution.py:156
  140.5 41.8 %last_update.1 = (f32[2,2,256,128]{3,2,1,0:T(8,128)S(1)}, f32[1024,128]{1,0:T(8,128)S(1)}) custom-call(f32[2,4,512,128]{3,2,1,0:T(8,128)S(1)} %get-tuple-element.18.acc, f32[2,4,512,128]{3,2,1,0:T(8,128)} %copy-done, f32[1024,128]{1,0:T(8,128)S(1)} %get-tuple-element.19.pacc, f32[1024,128]{1,0:T(8,128)S(1)} %get-tuple-element.17.probe.flat_old, ...), custom_call_target="tpu_custom_call" | custom-call | tf_op jit(solution)/shard_map/last_update/pallas_call | solution.py:513
  182.3 0.2 copy.14
  182.5 1.0 copy.16
  183.5 0.8 copy.27
  (7 shorter events, 0.0 us)
Async XLA Ops:
  3.7 1.0 copy-start.6
  4.7 1.0 copy-start.7
  27.4 1.3 copy-start.1
  28.7 1.0 copy-start.2
  29.8 1.0 copy-start.4
  57.8 55.4 %copy-start.3 = (bf16[512,512]{1,0:T(8,128)(2,1)S(1)}, bf16[512,512]{1,0:T(8,128)(2,1)}, u32[]{:S(2)}) copy-start(bf16[512,512]{1,0:T(8,128)(2,1)} %constant.16.clone.right) | copy-start | bytes 1572868
  57.8 55.4 %copy-start.5 = (bf16[512,512]{1,0:T(8,128)(2,1)S(1)}, bf16[512,512]{1,0:T(8,128)(2,1)}, u32[]{:S(2)}) copy-start(bf16[512,512]{1,0:T(8,128)(2,1)} %constant.15.clone.left) | copy-start | bytes 1572868
  111.8 1.3 copy-start

commit v2 on v1

v2 whole, which is shorter than its diff:
```python
import functools
import math

import jax
import jax.numpy as jnp
import ml_dtypes
import numpy as np
from jax import lax
from jax.experimental import pallas as pl
from jax.experimental.pallas import tpu as pltpu
from jax.sharding import PartitionSpec as P

W = 256
LANE = 128
H = W // 2
G = 2
VLIM = 32 * 2**20
ROWS = 8
COLS = 16
CHUNKS = 4
CH = W // CHUNKS
MESH = pl.DeviceIdType.MESH
F32 = jnp.float32
BF16 = jnp.bfloat16
VM = pl.BlockSpec(memory_space=pltpu.VMEM)
SM = pl.BlockSpec(memory_space=pltpu.SMEM)
ANY = pl.BlockSpec(memory_space=pl.ANY)
EXT = jax.ShapeDtypeStruct((2, 4, 2 * W, LANE), F32)
FLAT = jax.ShapeDtypeStruct((4 * W, LANE), F32)
TILE = jax.ShapeDtypeStruct((2, W, W), F32)
DMA = pltpu.SemaphoreType.DMA


def dft_tables():
    steps = np.arange(W)
    product = (steps[:, None] * steps[None, :]) % W
    angle = product.astype(np.float32) * np.float32(2.0 * math.pi / W)
    scale = np.float32(1.0 / math.sqrt(W))
    fr = (np.cos(angle) * scale).astype(ml_dtypes.bfloat16)
    fi = (-np.sin(angle) * scale).astype(ml_dtypes.bfloat16)
    order = np.concatenate([np.arange(0, W, 2), np.arange(1, W, 2)])
    left = np.block([[fr, -fi], [fi, fr]])[np.concatenate([order, order + W])]
    right = left.T
    right = np.concatenate([right[:, :H], right[:, W : W + H], right[:, H:W], right[:, W + H :]], axis=1)
    halves = []
    for odd in range(2):
        re, im = fr[odd::2, :H], fi[odd::2, :H]
        g = np.block([[re, -im], [im, re]])
        halves += [g, g.T]
    sort = np.zeros((W, W), np.float32)
    sort[np.arange(W), np.argsort(order)] = 1.0
    return np.ascontiguousarray(left), np.ascontiguousarray(right), np.stack(halves), sort.astype(ml_dtypes.bfloat16)


def dot(a, b):
    return jnp.dot(a, b, preferred_element_type=F32)


def window_kernel(pos, live, ext, probe, amps, ltab, rtab, tab, acc, pacc, win, ebuf, abuf, dbuf, bbuf, cbuf):
    slots = amps.shape[0]
    groups = slots // G

    def zero(i, _):
        rows = pl.ds(pl.multiple_of(i * 8, 8), 8)
        for part in range(2):
            for t in range(4):
                acc[part, t, rows, :] = jnp.zeros((8, LANE), F32)
        return 0

    lax.fori_loop(0, 64, zero, 0)

    def zero_probe(i, _):
        pacc[pl.ds(pl.multiple_of(i * 64, 64), 64), :] = jnp.zeros((64, LANE), F32)
        return 0

    lax.fori_loop(0, 16, zero_probe, 0)

    def zero_last(i, _):
        rows = pl.ds(pl.multiple_of(i * 16, 16), 16)
        for g in range(G):
            for part in range(2):
                win[1, g, part, rows, :] = jnp.zeros((16, W), F32)
                cbuf[1, g, part, rows, :] = jnp.zeros((16, W), F32)
        return 0

    lax.fori_loop(0, 16, zero_last, 0)
    B = 16
    lane = lax.broadcasted_iota(jnp.int32, (B, LANE), 1)

    def place_of(s):
        r = jnp.bitwise_and(pos[0, s], W - 1)
        c = jnp.bitwise_and(pos[1, s], W - 1)
        q = c // LANE
        return r, q, c - q * LANE

    def form(s, m, g, i):
        r, q, sh = place_of(s)
        keep = lane < LANE - sh
        o = i * B
        rows = pl.ds(o, B)
        w = []
        for part in range(2):
            cuts = [pltpu.roll(ext[part, q + u, pl.ds(r + o, B), :], LANE - sh, 1) for u in range(3)]
            w.append([jnp.where(keep, cuts[t], cuts[t + 1]) for t in range(2)])
        for t in range(2):
            cols = slice(t * LANE, (t + 1) * LANE)
            w0, w1 = w[0][t], w[1][t]
            win[m, g, 0, rows, cols] = w0
            win[m, g, 1, rows, cols] = w1
            pr = probe[pl.ds(t * W + o, B), :]
            pi = probe[pl.ds((2 + t) * W + o, B), :]
            ebuf[m, g, rows, cols] = (pr * w0 - pi * w1).astype(BF16)
            ebuf[m, g, pl.ds(W + o, B), cols] = (pr * w1 + pi * w0).astype(BF16)

    def left(m, g, half):
        x = dot(ltab[half * W : (half + 1) * W], ebuf[m, g]).astype(BF16)
        abuf[g, :, half * W : (half + 1) * W] = x

    def right(s, g, odd):
        on = s < live[0]
        y = dot(abuf[g], rtab[:, odd * W : (odd + 1) * W])
        for k in range(2):
            rows = slice(k * H, (k + 1) * H)
            yr, yi = y[rows, :H], y[rows, H:]
            amp = amps[s, rows, odd * H : (odd + 1) * H].astype(F32)
            f = amp * lax.rsqrt(jnp.maximum(yr * yr + yi * yi, 0.0625)) - 1.0
            f = jnp.where(on, f, 0.0)
            dbuf[g, k, :H, odd * H : (odd + 1) * H] = (f * yr).astype(BF16)
            dbuf[g, k, H:, odd * H : (odd + 1) * H] = (f * yi).astype(BF16)

    def unleft(g):
        be = dot(tab[1], dbuf[g, 0])
        bo = dot(tab[3], dbuf[g, 1])
        for sign in range(2):
            b = (be - bo if sign else be + bo).astype(BF16)
            rows = slice(sign * H, (sign + 1) * H)
            for odd in range(2):
                cols = slice(odd * H, (odd + 1) * H)
                bbuf[g, odd, rows, :H] = b[:H, cols]
                bbuf[g, odd, rows, H:] = b[H:, cols]

    def unright(m, g, odd):
        cbuf[m, g, odd] = dot(bbuf[g, odd], tab[2 * odd])

    def put(s, m, g, i):
        r, q, sh = place_of(s)
        keep = lane >= sh
        o = i * B
        rows = pl.ds(o, B)
        terms = [[], []]
        er, ei = cbuf[m, g, 0, rows, :H], cbuf[m, g, 0, rows, H:]
        dr, di = cbuf[m, g, 1, rows, :H], cbuf[m, g, 1, rows, H:]
        for t in range(2):
            cols = slice(t * LANE, (t + 1) * LANE)
            at_re = pl.ds(t * W + o, B)
            at_im = pl.ds((2 + t) * W + o, B)
            pr = probe[at_re, :]
            pi = probe[at_im, :]
            cr, ci = (er - dr, ei - di) if t else (er + dr, ei + di)
            wr = win[m, g, 0, rows, cols]
            wi = win[m, g, 1, rows, cols]
            pacc[at_re, :] += wr * cr + wi * ci
            pacc[at_im, :] += wr * ci - wi * cr
            terms[0].append(pltpu.roll(pr * cr + pi * ci, sh, 1))
            terms[1].append(pltpu.roll(pr * ci - pi * cr, sh, 1))
        at = pl.ds(r + o, B)
        for part in range(2):
            a, b = terms[part]
            acc[part, q, at, :] += jnp.where(keep, a, 0.0)
            acc[part, q + 1, at, :] += jnp.where(keep, b, a)
            acc[part, q + 2, at, :] += jnp.where(keep, 0.0, b)

    def stage(p, m):
        before = jnp.maximum(p - 1, 0)
        after = jnp.minimum(p + 1, groups - 1)
        main = []
        for g in range(G):
            main += [lambda g=g, h=h: left(m, g, h) for h in range(2)]
        for g in range(G):
            main += [lambda g=g, h=h: right(p * G + g, g, h) for h in range(2)]
        for g in range(G):
            main += [lambda g=g: unleft(g)]
        for g in range(G):
            main += [lambda g=g, h=h: unright(m, g, h) for h in range(2)]
        side = []
        for g in range(G):
            for i in range(W // B):
                side += [lambda g=g, i=i: put(before * G + g, 1 - m, g, i), lambda g=g, i=i: form(after * G + g, 1 - m, g, i)]
        done = 0
        for n, work in enumerate(main):
            work()
            upto = len(side) * (n + 1) // len(main)
            for extra in side[done:upto]:
                extra()
            done = upto

    for g in range(G):
        for i in range(W // B):
            form(g, 0, g, i)

    def step(p, _):
        stage(2 * p, 0)
        stage(2 * p + 1, 1)
        return 0

    lax.fori_loop(0, groups // 2, step, 0)
    for g in range(G):
        for i in range(W // B):
            put(slots - G + g, 1, g, i)


def window_call(places, live, ext, probe, amps, ltab, rtab, tab):
    return pl.pallas_call(
        window_kernel,
        out_shape=(EXT, FLAT),
        in_specs=[SM, SM, VM, VM, VM, VM, VM, VM],
        out_specs=(VM, VM),
        scratch_shapes=[
            pltpu.VMEM((2, G, 2, W, W), F32),
            pltpu.VMEM((2, G, 2 * W, W), BF16),
            pltpu.VMEM((G, W, 2 * W), BF16),
            pltpu.VMEM((G, 2, W, W), BF16),
            pltpu.VMEM((G, 2, W, W), BF16),
            pltpu.VMEM((2, G, 2, W, W), F32),
        ],
        compiler_params=pltpu.CompilerParams(vmem_limit_bytes=VLIM),
        name="windows",
    )(places, live, ext, probe, amps, ltab, rtab, tab)


def remote(src, dst, send, recv, to):
    return pltpu.make_async_remote_copy(
        src_ref=src, dst_ref=dst, send_sem=send, recv_sem=recv, device_id=to, device_id_type=MESH
    )


def where_am_i():
    row = lax.axis_index("row")
    col = lax.axis_index("col")
    up = (lax.rem(row + ROWS - 1, ROWS), col)
    down = (lax.rem(row + 1, ROWS), col)
    west = (row, lax.rem(col + COLS - 1, COLS))
    east = (row, lax.rem(col + 1, COLS))
    return row, col, up, down, west, east


def greet(targets):
    barrier = pltpu.get_barrier_semaphore()
    for target in targets:
        pl.semaphore_signal(barrier, inc=1, device_id=target, device_id_type=MESH)
    pl.semaphore_wait(barrier, len(targets))


def chunk(k, base=0):
    return pl.ds(base + k * CH, CH)


def halo_copies(tile, ext, send, recv, west, up):
    far = pl.ds(2, 2)
    to_west = [remote(tile(k), ext.at[:, far, chunk(k), :], send.at[k], recv.at[k], west) for k in range(CHUNKS)]
    base = CHUNKS
    to_up = [
        remote(tile(k), ext.at[:, pl.ds(0, 2), chunk(k, W), :], send.at[base + k], recv.at[base + k], up)
        for k in range(CHUNKS)
    ]
    base = 2 * CHUNKS
    onward = [
        remote(
            ext.at[:, far, chunk(k), :], ext.at[:, far, chunk(k, W), :], send.at[base + k], recv.at[base + k], up
        )
        for k in range(CHUNKS)
    ]
    return to_west, to_up, onward


def halo_finish(copies):
    to_west, to_up, onward = copies
    for first, second in zip(to_west, onward):
        first.wait_recv()
        second.start()
    for copy in [*to_up, *onward]:
        copy.wait_recv()
    for copy in [*to_west, *to_up, *onward]:
        copy.wait_send()


HALO_SEMS = 3 * CHUNKS


def halo_kernel(obj, probe, amps, sort, ext, flat, amps_out, amps_in, send, recv, local, amp_sem):
    row, col, up, down, west, east = where_am_i()
    slots = amps.shape[0]
    inward = [
        pltpu.make_async_copy(obj.at[:, :, pl.ds(t * LANE, LANE)], ext.at[:, t, pl.ds(0, W), :], local.at[t])
        for t in range(2)
    ]
    fill = pltpu.make_async_copy(amps, amps_in, amp_sem)
    lay = [
        pltpu.make_async_copy(
            probe.at[part, :, pl.ds(t * LANE, LANE)],
            flat.at[pl.ds((part * 2 + t) * W, W), :],
            local.at[2 + part * 2 + t],
        )
        for part in range(2)
        for t in range(2)
    ]
    for copy in [*inward, fill, *lay]:
        copy.start()
    greet([up, down, west, east])
    inward[0].wait()
    inward[1].wait()
    copies = halo_copies(lambda k: ext.at[:, pl.ds(0, 2), chunk(k), :], ext, send, recv, west, up)
    for copy in copies[0]:
        copy.start()
    for copy in copies[1]:
        copy.start()
    fill.wait()

    def reorder(s, _):
        rows = lax.dot_general(sort[...], amps_in[s], (((0,), (0,)), ((), ())), preferred_element_type=F32)
        amps_out[s] = dot(rows.astype(BF16), sort[...]).astype(BF16)
        return 0

    lax.fori_loop(0, slots, reorder, 0)
    for copy in lay:
        copy.wait()
    halo_finish(copies)


def halo_call(obj, probe, amps, sort):
    return pl.pallas_call(
        halo_kernel,
        out_shape=(EXT, FLAT, jax.ShapeDtypeStruct(amps.shape, BF16)),
        in_specs=[ANY, ANY, ANY, VM],
        out_specs=(VM, VM, VM),
        scratch_shapes=[
            pltpu.VMEM(amps.shape, BF16),
            DMA((HALO_SEMS,)),
            DMA((HALO_SEMS,)),
            DMA((6,)),
            DMA,
        ],
        compiler_params=pltpu.CompilerParams(collective_id=0, has_side_effects=True, vmem_limit_bytes=VLIM),
        name="first_halo",
    )(obj, probe, amps, sort)


TOP = 16
FRAME = W + 2 * TOP


def correlate_block(v, o, kernel, slabs, lane):
    sums = []
    for t in range(3):
        above, here, below = (v(t, o + a) for a in (-1, 0, 1))
        sums.append([above * kernel(0, b) + here * kernel(1, b) + below * kernel(2, b) for b in range(3)])
    before = [pltpu.roll(sums[t][0], 1, 1) for t in range(3)]
    after = [pltpu.roll(sums[t][2], LANE - 1, 1) for t in range(3)]
    return [
        sums[t][1]
        + jnp.where(lane == 0, before[(t + 2) % 3], before[t])
        + jnp.where(lane == LANE - 1, after[(t + 1) % 3], after[t])
        for t in slabs
    ]


def update_kernel(
    step, last, acc, ext_old, pacc, flat_old, kernel_first, kernel_second, ext, flat,
    from_up, from_west, onward, rim_out, rim_in, frame, real,
    p1, h1, p2, h2, p3,
    y_send, y_recv, x_send, x_recv, rim_send, rim_recv, h_send, h_recv,
    a_send, a_recv, b_send, b_recv, c_send, c_recv, d_send, d_recv,
):
    row, col, up, down, west, east = where_am_i()
    core = lax.rem(row, 2)
    y = row // 2
    mate = (row + 1 - 2 * core, col)
    beyond = (lax.rem(row + ROWS - 1 + 2 * core, ROWS), col)
    in_y = [(lax.rem(row + 2 * d, ROWS), col) for d in range(1, 4)]
    in_col = [(row, lax.rem(col + d, COLS)) for d in range(1, COLS)]
    greet([mate, beyond, *in_y, *in_col])

    y_copies = [
        remote(acc.at[:, pl.ds(2, 2), chunk(k, W), :], from_up.at[:, pl.ds(2, 2), chunk(k), :], y_send.at[k], y_recv.at[k], down)
        for k in range(CHUNKS)
    ]
    y_copies.append(
        remote(acc.at[:, pl.ds(0, 2), pl.ds(W, W), :], from_up.at[:, pl.ds(0, 2), :, :], y_send.at[CHUNKS], y_recv.at[CHUNKS], down)
    )
    for copy in y_copies:
        copy.start()

    mine = pl.multiple_of(core * 512, 512)
    other = pl.multiple_of(512 - core * 512, 512)
    a_copies = [remote(pacc.at[pl.ds(other, 512), :], p1, a_send.at[0], a_recv.at[0], mate)]
    a_copies[0].start()

    x_copies = []
    for k in range(CHUNKS):
        y_copies[k].wait_recv()

        def join(i, _):
            o = pl.multiple_of(i * 16, 16)
            for part in range(2):
                for t in range(2):
                    onward[part, t, pl.ds(k * CH + o, 16), :] = (
                        acc[part, 2 + t, pl.ds(k * CH + o, 16), :] + from_up[part, 2 + t, pl.ds(k * CH + o, 16), :]
                    )
            return 0

        lax.fori_loop(0, CH // 16, join, 0)
        copy = remote(onward.at[:, :, chunk(k), :], from_west.at[:, :, chunk(k), :], x_send.at[k], x_recv.at[k], east)
        copy.start()
        x_copies.append(copy)

    a_copies[0].wait_recv()

    def join_half(i, _):
        o = pl.multiple_of(i * 64, 64)
        h1[pl.ds(o, 64), :] = pacc[pl.ds(mine + o, 64), :] + p1[pl.ds(o, 64), :]
        return 0

    lax.fori_loop(0, 8, join_half, 0)
    b_copies = []
    for d in range(1, 4):
        block = pl.multiple_of(lax.rem(y + d, 4) * LANE, LANE)
        b_copies.append(remote(h1.at[pl.ds(block, LANE), :], p2.at[d - 1], b_send.at[d - 1], b_recv.at[d - 1], in_y[d - 1]))
    for copy in b_copies:
        copy.start()

    for t in range(3):
        for part in range(2):
            frame[part, t, pl.ds(0, 8), :] = jnp.zeros((8, LANE), F32)
            frame[part, t, pl.ds(FRAME - 8, 8), :] = jnp.zeros((8, LANE), F32)

    def step_rows(k):
        def add(i, _):
            o = pl.multiple_of(k * CH + i * 16, 16)
            rows = pl.ds(o, 16)
            for part in range(2):
                for t in range(2):
                    total = acc[part, t, rows, :] + from_up[part, t, rows, :] + from_west[part, t, rows, :]
                    frame[part, 1 + t, pl.ds(TOP + o, 16), :] = ext_old[part, t, rows, :] + total * (1.0 / 16.0)
            return 0

        lax.fori_loop(0, CH // 16, add, 0)

    y_copies[CHUNKS].wait_recv()
    for k in range(CHUNKS // 2):
        x_copies[k].wait_recv()
        step_rows(k)

    for copy in b_copies:
        copy.wait_recv()
    here = pl.multiple_of(y * LANE, LANE)
    h2[...] = h1[pl.ds(here, LANE), :] + p2[0] + p2[1] + p2[2]
    c_copies = []
    for d in range(1, COLS):
        block = pl.multiple_of(lax.rem(col + d, COLS) * 8, 8)
        c_copies.append(remote(h2.at[pl.ds(block, 8), :], p3.at[d], c_send.at[d], c_recv.at[d], in_col[d - 1]))
    for copy in c_copies:
        copy.start()

    for k in range(CHUNKS // 2, CHUNKS):
        x_copies[k].wait_recv()
        step_rows(k)

    side = lax.broadcasted_iota(jnp.int32, (W, LANE), 1) < LANE // 2
    for part in range(2):
        ends = jnp.where(side, frame[part, 1, pl.ds(TOP, W), :], frame[part, 2, pl.ds(TOP, W), :]).T
        rim_out[0, part, :, :] = ends[:8, :]
        rim_out[1, part, :, :] = ends[LANE - 8 :, :]
    rims = [
        remote(rim_out.at[0], rim_in.at[0], rim_send.at[0], rim_recv.at[0], west),
        remote(rim_out.at[1], rim_in.at[1], rim_send.at[1], rim_recv.at[1], east),
    ]
    rims[0].start()
    rims[1].start()

    for copy in c_copies:
        copy.wait_recv()
    own = pl.multiple_of(col * 8, 8)
    total = h2[pl.ds(own, 8), :]
    for d in range(1, COLS):
        total = total + p3[d]
    piece = pl.multiple_of(core * 512 + y * LANE + col * 8, 8)
    flat[pl.ds(piece, 8), :] = flat_old[pl.ds(piece, 8), :] + total * (2.0 / math.sqrt(2048.0))
    d_copies = []
    for d in range(1, COLS):
        d_copies.append(
            remote(flat.at[pl.ds(piece, 8), :], flat.at[pl.ds(piece, 8), :], d_send.at[d], d_recv.at[d], in_col[d - 1])
        )
    for copy in d_copies:
        copy.start()

    rims[0].wait_recv()
    rims[1].wait_recv()
    blank = jnp.zeros((LANE - 16, W), F32)
    for part in range(2):
        right_rim = jnp.where(col < COLS - 1, rim_in[0, part, :, :], 0.0)
        left_rim = jnp.where(col > 0, rim_in[1, part, :, :], 0.0)
        frame[part, 0, pl.ds(TOP, W), :] = jnp.concatenate([right_rim, blank, left_rim], axis=0).T
    rows_out = [
        remote(frame.at[:, :, pl.ds(TOP, 8), :], frame.at[:, :, pl.ds(TOP + W, 8), :], rim_send.at[2], rim_recv.at[2], up),
        remote(frame.at[:, :, pl.ds(TOP + W - 8, 8), :], frame.at[:, :, pl.ds(TOP - 8, 8), :], rim_send.at[3], rim_recv.at[3], down),
    ]
    rows_out[0].start()
    rows_out[1].start()

    def gathered(first, count, send, recv, to):
        return remote(flat.at[pl.ds(first, count), :], flat.at[pl.ds(first, count), :], send, recv, to)

    for copy in d_copies:
        copy.wait_recv()
    quarter = pl.multiple_of(core * 512 + y * LANE, LANE)
    for d in range(1, 4):
        b_copies.append(gathered(quarter, LANE, b_send.at[2 + d], b_recv.at[2 + d], in_y[d - 1]))
        b_copies[-1].start()

    rows_out[0].wait_recv()
    rows_out[1].wait_recv()
    for part in range(2):
        for t in range(3):
            top = pl.ds(TOP - 8, 8)
            low = pl.ds(TOP + W, 8)
            frame[part, t, top, :] = jnp.where(row > 0, frame[part, t, top, :], 0.0)
            frame[part, t, low, :] = jnp.where(row < ROWS - 1, frame[part, t, low, :], 0.0)

    lane8 = lax.broadcasted_iota(jnp.int32, (8, LANE), 1)
    lane32 = lax.broadcasted_iota(jnp.int32, (32, LANE), 1)
    west_on = (col > 0).astype(F32)
    east_on = (col < COLS - 1).astype(F32)

    def tap(ref):
        return lambda a, b: ref[a, step, b]

    def first(o, count, lane, keep):
        parts = correlate_block(lambda t, at: frame[1, t, pl.ds(at, count), :], o, tap(kernel_first), range(3), lane)
        for t in range(3):
            value = frame[0, t, pl.ds(o, count), :] + jnp.tanh(parts[t])
            if t == 0:
                value = value * jnp.where(lane < LANE // 2, east_on, west_on)
            if keep is not None:
                value = value * keep
            real[t, pl.ds(o, count), :] = value

    first(TOP - 8, 8, lane8, (row > 0).astype(F32))
    first(TOP + W, 8, lane8, (row < ROWS - 1).astype(F32))

    def first_rows(i, _):
        first(pl.multiple_of(TOP + i * 32, 16), 32, lane32, None)
        return 0

    lax.fori_loop(0, W // 32, first_rows, 0)

    def second(i):
        o = pl.multiple_of(TOP + i * 32, 16)
        at = pl.ds(pl.multiple_of(i * 32, 32), 32)
        parts = correlate_block(lambda t, a: real[t, pl.ds(a, 32), :], o, tap(kernel_second), range(1, 3), lane32)
        for t in range(2):
            new_re = real[1 + t, pl.ds(o, 32), :]
            new_im = frame[1, 1 + t, pl.ds(o, 32), :] + jnp.tanh(parts[t])
            if last:
                ext[0, at, t * LANE : (t + 1) * LANE] = new_re
                ext[1, at, t * LANE : (t + 1) * LANE] = new_im
            else:
                ext[0, t, at, :] = new_re
                ext[1, t, at, :] = new_im

    def second_rows(i, _):
        second(i)
        return 0

    if not last:
        copies = halo_copies(lambda k: ext.at[:, pl.ds(0, 2), chunk(k), :], ext, h_send, h_recv, west, up)
    for k in range(CHUNKS):
        lax.fori_loop(k * CH // 32, (k + 1) * CH // 32, second_rows, 0)
        if not last:
            copies[0][k].start()
            copies[1][k].start()

    for copy in b_copies[3:]:
        copy.wait_recv()
    a_copies.append(gathered(mine, 512, a_send.at[1], a_recv.at[1], mate))
    a_copies[1].start()
    if not last:
        halo_finish(copies)
    a_copies[1].wait_recv()
    for copy in [*y_copies, *x_copies, *a_copies, *b_copies, *c_copies, *d_copies, *rims, *rows_out]:
        copy.wait_send()


def update_call(step, last, acc, ext, pacc, flat, kernel_first, kernel_second):
    return pl.pallas_call(
        functools.partial(update_kernel, step, last),
        out_shape=(TILE if last else EXT, FLAT),
        in_specs=[VM, VM, VM, VM, SM, SM],
        out_specs=(VM, VM),
        scratch_shapes=[
            pltpu.VMEM((2, 4, W, LANE), F32),
            pltpu.VMEM((2, 2, W, LANE), F32),
            pltpu.VMEM((2, 2, W, LANE), F32),
            pltpu.VMEM((2, 2, 8, W), F32),
            pltpu.VMEM((2, 2, 8, W), F32),
            pltpu.VMEM((2, 3, FRAME, LANE), F32),
            pltpu.VMEM((3, FRAME, LANE), F32),
            pltpu.VMEM((512, LANE), F32),
            pltpu.VMEM((512, LANE), F32),
            pltpu.VMEM((3, LANE, LANE), F32),
            pltpu.VMEM((LANE, LANE), F32),
            pltpu.VMEM((COLS, 8, LANE), F32),
            DMA((CHUNKS + 1,)), DMA((CHUNKS + 1,)),
            DMA((CHUNKS,)), DMA((CHUNKS,)),
            DMA((4,)), DMA((4,)),
            DMA((HALO_SEMS,)), DMA((HALO_SEMS,)),
            DMA((2,)), DMA((2,)),
            DMA((6,)), DMA((6,)),
            DMA((COLS,)), DMA((COLS,)),
            DMA((COLS,)), DMA((COLS,)),
        ],
        compiler_params=pltpu.CompilerParams(
            collective_id=2 if last else 1, has_side_effects=True, vmem_limit_bytes=VLIM
        ),
        name="last_update" if last else "update",
    )(acc, ext, pacc, flat, kernel_first, kernel_second)


def body(object_field, probe, positions, amplitudes, live, kernel_first, kernel_second):
    ltab, rtab, tab, sort = (jnp.asarray(table) for table in dft_tables())
    places = positions.T
    kernel_first = kernel_first.transpose(1, 0, 2)
    kernel_second = kernel_second.transpose(1, 0, 2)
    iters = kernel_first.shape[1]
    ext, flat, amps = halo_call(object_field, probe, amplitudes, sort)
    for step in range(iters):
        acc, pacc = window_call(places, live, ext, flat, amps, ltab, rtab, tab)
        ext, flat = update_call(step, step == iters - 1, acc, ext, pacc, flat, kernel_first, kernel_second)
    return ext, flat.reshape(2, 2, W, LANE).transpose(0, 2, 1, 3).reshape(2, W, W)


def solution(mesh):
    return jax.shard_map(
        body,
        mesh=mesh,
        in_specs=(
            P(None, "row", "col"),
            P(),
            P(("row", "col"), None),
            P(("row", "col"), None, None),
            P(("row", "col")),
            P(),
            P(),
        ),
        out_specs=(P(None, "row", "col"), P()),
        check_vma=False,
    )
```

time: 185 us -> 151 us (0.82)
  Pallas kernels: 172 us -> 143 us
  local copies, waits for them, and re-layouts: 11.1 us -> 6.22 us
    pallas_call x2, Pallas kernels: 54.3 us -> 32 us  [window_call(): pl.pallas_call(window_kernel, out_shape=(EXT, FLAT), in_specs=[SM, SM, VM...]
    pallas_call x3, Pallas kernels: 117 us -> 111 us  [the longest x2 89.4 us: update_call(): pl.pallas_call(functools.partial(update_kernel, step, last), out_shape=(T...]
    unnamed x20 -> x21, local copies, waits for them, and re-layouts: 8.58 us -> 5.39 us
where the time goes in v2:
time: 151 us
  Pallas kernels  143 us (95%)
  local copies, waits for them, and re-layouts  6.22 us (4%)
    pallas_call x2, Pallas kernels, update_call(): pl.pallas_call(functools.partial(update_kernel, step, last), out_shape=(T...  89.4 us
    pallas_call x2, Pallas kernels, window_call(): pl.pallas_call(window_kernel, out_shape=(EXT, FLAT), in_specs=[SM, SM, VM...  32 us
    pallas_call x1, Pallas kernels, halo_call(): pl.pallas_call(halo_kernel, out_shape=(EXT, FLAT, jax.ShapeDtypeStruct(am...  22.1 us
    unnamed x21, local copies, waits for them, and re-layouts  5.39 us

profile of v2, /device:TPU:1, one launch (start us, length us, event | category | flops | bytes accessed | tf_op | source)
XLA Modules:
  0.0 151.1 jit_solution(2510969301426754815)
XLA Ops:
  0.6 0.0 copy-start.9
  1.3 0.0 copy-start
  1.3 1.6 %copy-done = bf16[16,256,256]{2,1,0:T(8,128)(2,1)S(1)} copy-done((bf16[16,256,256]{2,1,0:T(8,128)(2,1)S(1)}, bf16[16,256,256]{2,1,0:T(8,128)(2,1)}, u32[]{:S(2)}) %copy-start) | copy-done | bytes 2097176
  2.9 0.0 copy-start.4
  2.9 1.0 copy-done.4
  3.9 0.0 copy-start.5
  3.9 1.0 copy-done.5
  5.0 0.0 copy-start.6
  5.0 0.9 copy-done.6
  5.9 22.1 %first_halo.1 = (f32[2,4,512,128]{3,2,1,0:T(8,128)S(1)}, f32[1024,128]{1,0:T(8,128)S(1)}, bf16[16,256,256]{2,1,0:T(8,128)(2,1)S(1)}) custom-call(f32[2,256,256]{2,1,0:T(8,128)S(1)} %copy-done.4, f32[2,256,256]{2,1,0:T(8,128)S(1)} %copy-done.5, bf16[16,256,256]{2,1,0:T(8,128)(2,1)S(1)} %copy-done, bf16[256,256]{1,0:T(8,128)(2,1)S(1)} %copy-done.6), custom_call_target="tpu_custom_call" | custom-call | tf_op jit(solution)/shard_map/first_halo/pallas_call | solution.py:331
  28.0 0.0 copy-done.9
  28.0 0.0 copy-done.1
  28.0 0.0 copy-done.2
  28.0 0.0 copy-done.3
  28.0 0.0 copy-start.7
  28.1 0.0 copy-start.8
  28.1 15.9 %windows.2 = (f32[2,4,512,128]{3,2,1,0:T(8,128)S(1)}, f32[1024,128]{1,0:T(8,128)S(1)}) custom-call(s32[2,16]{1,0:T(2,128)S(1)} %bitcast.15, s32[1]{0:T(128)S(6)} %copy.18.live, f32[2,4,512,128]{3,2,1,0:T(8,128)S(1)} %get-tuple-element.13.ext.ext_old, f32[1024,128]{1,0:T(8,128)S(1)} %get-tuple-element.14.probe.flat_old, ...), custom_call_target="tpu_custom_call" | custom-call | tf_op jit(solution)/shard_map/windows/pallas_call | solution.py:213
  44.0 0.0 copy-done.7
  44.0 0.0 copy-done.8
  44.0 49.4 %update.1 = (f32[2,4,512,128]{3,2,1,0:T(8,128)S(1)}, f32[1024,128]{1,0:T(8,128)S(1)}) custom-call(f32[2,4,512,128]{3,2,1,0:T(8,128)S(1)} %get-tuple-element.16.acc, f32[2,4,512,128]{3,2,1,0:T(8,128)S(1)} %get-tuple-element.13.ext.ext_old, f32[1024,128]{1,0:T(8,128)S(1)} %get-tuple-element.17.pacc, f32[1024,128]{1,0:T(8,128)S(1)} %get-tuple-element.14.probe.flat_old, ...), custom_call_target="tpu_custom_call" | custom-call | tf_op jit(solution)/shard_map/update/pallas_call | solution.py:594
  93.4 16.1 %windows.3 = (f32[2,4,512,128]{3,2,1,0:T(8,128)S(1)}, f32[1024,128]{1,0:T(8,128)S(1)}) custom-call(s32[2,16]{1,0:T(2,128)S(1)} %bitcast.16, s32[1]{0:T(128)S(6)} %copy.18.live, f32[2,4,512,128]{3,2,1,0:T(8,128)S(1)} %get-tuple-element.18.ext.ext_old, f32[1024,128]{1,0:T(8,128)S(1)} %get-tuple-element.19.probe.flat_old, ...), custom_call_target="tpu_custom_call" | custom-call | tf_op jit(solution)/shard_map/windows/pallas_call | solution.py:213
  109.5 40.0 %last_update.1 = (f32[2,256,256]{2,1,0:T(8,128)S(1)}, f32[1024,128]{1,0:T(8,128)S(1)}) custom-call(f32[2,4,512,128]{3,2,1,0:T(8,128)S(1)} %get-tuple-element.20.acc, f32[2,4,512,128]{3,2,1,0:T(8,128)S(1)} %get-tuple-element.18.ext.ext_old, f32[1024,128]{1,0:T(8,128)S(1)} %get-tuple-element.21.pacc, f32[1024,128]{1,0:T(8,128)S(1)} %get-tuple-element.19.probe.flat_old, ...), custom_call_target="tpu_custom_call" | custom-call | tf_op jit(solution)/shard_map/last_update/pallas_call | solution.py:594
  149.4 0.8 copy.16
  150.3 0.8 copy.19
  (3 shorter events, 0.0 us)
Async XLA Ops:
  0.6 27.4 %copy-start.9 = (s32[16,2]{0,1:T(2,128)S(1)}, s32[16,2]{0,1:T(2,128)}, u32[]{:S(2)}) copy-start(s32[16,2]{0,1:T(2,128)} %param.13) | copy-start | bytes 388
  1.3 1.6 %copy-start = (bf16[16,256,256]{2,1,0:T(8,128)(2,1)S(1)}, bf16[16,256,256]{2,1,0:T(8,128)(2,1)}, u32[]{:S(2)}) copy-start(bf16[16,256,256]{2,1,0:T(8,128)(2,1)} %amps.1) | copy-start | bytes 6291460
  2.9 1.0 copy-start.4
  3.9 1.0 copy-start.5
  5.0 0.9 copy-start.6
  5.9 22.1 %copy-start.1 = (bf16[4,256,256]{2,1,0:T(8,128)(2,1)S(1)}, bf16[4,256,256]{2,1,0:T(8,128)(2,1)}, u32[]{:S(2)}) copy-start(bf16[4,256,256]{2,1,0:T(8,128)(2,1)} %constant.10.clone.tab) | copy-start | bytes 1572868
  5.9 22.1 %copy-start.2 = (bf16[512,512]{1,0:T(8,128)(2,1)S(1)}, bf16[512,512]{1,0:T(8,128)(2,1)}, u32[]{:S(2)}) copy-start(bf16[512,512]{1,0:T(8,128)(2,1)} %constant.9.clone.rtab) | copy-start | bytes 1572868
  5.9 22.1 %copy-start.3 = (bf16[512,512]{1,0:T(8,128)(2,1)S(1)}, bf16[512,512]{1,0:T(8,128)(2,1)}, u32[]{:S(2)}) copy-start(bf16[512,512]{1,0:T(8,128)(2,1)} %constant.8.clone.ltab) | copy-start | bytes 1572868
  28.0 16.0 %copy-start.7 = (f32[2,3,3]{2,0,1:T(2,128)S(1)}, f32[2,3,3]{2,0,1:T(2,128)}, u32[]{:S(2)}) copy-start(f32[2,3,3]{2,0,1:T(2,128)} %param.16) | copy-start | bytes 220
  28.1 15.9 %copy-start.8 = (f32[2,3,3]{2,0,1:T(2,128)S(1)}, f32[2,3,3]{2,0,1:T(2,128)}, u32[]{:S(2)}) copy-start(f32[2,3,3]{2,0,1:T(2,128)} %param.17) | copy-start | bytes 220

commit v3 on v2

--- a/solution.py
+++ b/solution.py
@@ -17,8 +17,10 @@
 VLIM = 32 * 2**20
 ROWS = 8
 COLS = 16
-CHUNKS = 4
-CH = W // CHUNKS
+SPILL = (8, 96, 176, 224, 248)
+FIRST = (0, 32, 64, 96, 128, 160, 192, 224, 256)
+REAL = (0, 80, 160, 208, 256)
+LATER = (0, 64, 128, 192, 256)
 MESH = pl.DeviceIdType.MESH
 F32 = jnp.float32
 BF16 = jnp.bfloat16
@@ -251,40 +253,51 @@
     pl.semaphore_wait(barrier, len(targets))
 
 
-def chunk(k, base=0):
-    return pl.ds(base + k * CH, CH)
-
-
-def halo_copies(tile, ext, send, recv, west, up):
-    far = pl.ds(2, 2)
-    to_west = [remote(tile(k), ext.at[:, far, chunk(k), :], send.at[k], recv.at[k], west) for k in range(CHUNKS)]
-    base = CHUNKS
-    to_up = [
-        remote(tile(k), ext.at[:, pl.ds(0, 2), chunk(k, W), :], send.at[base + k], recv.at[base + k], up)
-        for k in range(CHUNKS)
-    ]
-    base = 2 * CHUNKS
-    onward = [
-        remote(
-            ext.at[:, far, chunk(k), :], ext.at[:, far, chunk(k, W), :], send.at[base + k], recv.at[base + k], up
-        )
-        for k in range(CHUNKS)
-    ]
+def pieces(bounds, base=0):
+    return [pl.ds(base + first, end - first) for first, end in zip(bounds, bounds[1:])]
+
+
+class Copy:
+    def __init__(self, made):
+        self.made, self.left = made, False
+        self.start, self.wait_recv = made.start, made.wait_recv
+
+    def wait_send(self):
+        if not self.left:
+            self.left = True
+            self.made.wait_send()
+
+
+class Links:
+    def __init__(self, send, recv):
+        self.send, self.recv, self.copies = send, recv, []
+
+    def copy(self, src, dst, to):
+        at = len(self.copies)
+        self.copies.append(Copy(remote(src, dst, self.send.at[at], self.recv.at[at], to)))
+        return self.copies[-1]
+
+    def start(self, src, dst, to):
+        made = self.copy(src, dst, to)
+        made.start()
+        return made
+
+    def drain(self):
+        for made in self.copies:
+            made.wait_send()
+
+
+def halo_copies(links, ext, bounds, west, up):
+    near, far = pl.ds(0, 2), pl.ds(2, 2)
+    high, low = pieces(bounds), pieces(bounds, W)
+    to_west = [links.copy(ext.at[:, near, a, :], ext.at[:, far, a, :], west) for a in high]
+    to_up = [links.copy(ext.at[:, near, a, :], ext.at[:, near, b, :], up) for a, b in zip(high, low)]
+    onward = [links.copy(ext.at[:, far, a, :], ext.at[:, far, b, :], up) for a, b in zip(high, low)]
     return to_west, to_up, onward
 
 
-def halo_finish(copies):
-    to_west, to_up, onward = copies
-    for first, second in zip(to_west, onward):
-        first.wait_recv()
-        second.start()
-    for copy in [*to_up, *onward]:
-        copy.wait_recv()
-    for copy in [*to_west, *to_up, *onward]:
-        copy.wait_send()
-
-
-HALO_SEMS = 3 * CHUNKS
+HALO_SEMS = 3 * (len(FIRST) - 1)
+UPDATE_SEMS = 96
 
 
 def halo_kernel(obj, probe, amps, sort, ext, flat, amps_out, amps_in, send, recv, local, amp_sem):
@@ -309,22 +322,41 @@
     greet([up, down, west, east])
     inward[0].wait()
     inward[1].wait()
-    copies = halo_copies(lambda k: ext.at[:, pl.ds(0, 2), chunk(k), :], ext, send, recv, west, up)
-    for copy in copies[0]:
-        copy.start()
-    for copy in copies[1]:
-        copy.start()
+    links = Links(send, recv)
+    copies = halo_copies(links, ext, FIRST, west, up)
+    to_west, to_up, onward = copies
+    ahead = 4
+    for k in range(ahead):
+        to_west[k].start()
+    to_up[0].start()
+    to_up[1].start()
     fill.wait()
 
-    def reorder(s, _):
+    def reorder(s):
         rows = lax.dot_general(sort[...], amps_in[s], (((0,), (0,)), ((), ())), preferred_element_type=F32)
         amps_out[s] = dot(rows.astype(BF16), sort[...]).astype(BF16)
-        return 0
-
-    lax.fori_loop(0, slots, reorder, 0)
+
+    def reorder_some(first, last):
+        def one(s, _):
+            reorder(s)
+            return 0
+
+        lax.fori_loop(first, last, one, 0)
+
+    count = len(to_west)
+    for k in range(count):
+        reorder_some(k * slots // count, (k + 1) * slots // count)
+        to_west[k].wait_recv()
+        onward[k].start()
+        if k + ahead < count:
+            to_west[k + ahead].start()
+        if k + 2 < count:
+            to_up[k + 2].start()
+    for copy in [*to_up, *onward]:
+        copy.wait_recv()
     for copy in lay:
         copy.wait()
-    halo_finish(copies)
+    links.drain()
 
 
 def halo_call(obj, probe, amps, sort):
@@ -366,10 +398,8 @@
 
 def update_kernel(
     step, last, acc, ext_old, pacc, flat_old, kernel_first, kernel_second, ext, flat,
-    from_up, from_west, onward, rim_out, rim_in, frame, real,
-    p1, h1, p2, h2, p3,
-    y_send, y_recv, x_send, x_recv, rim_send, rim_recv, h_send, h_recv,
-    a_send, a_recv, b_send, b_recv, c_send, c_recv, d_send, d_recv,
+    from_up, from_west, onward, strip, strip_up, strip_west, strip_on, strip_new, rim_in, corner_in, frame, real,
+    p1, h1, p2, h3, p4, send, recv,
 ):
     row, col, up, down, west, east = where_am_i()
     core = lax.rem(row, 2)
@@ -378,42 +408,67 @@
     beyond = (lax.rem(row + ROWS - 1 + 2 * core, ROWS), col)
     in_y = [(lax.rem(row + 2 * d, ROWS), col) for d in range(1, 4)]
     in_col = [(row, lax.rem(col + d, COLS)) for d in range(1, COLS)]
-    greet([mate, beyond, *in_y, *in_col])
-
-    y_copies = [
-        remote(acc.at[:, pl.ds(2, 2), chunk(k, W), :], from_up.at[:, pl.ds(2, 2), chunk(k), :], y_send.at[k], y_recv.at[k], down)
-        for k in range(CHUNKS)
-    ]
-    y_copies.append(
-        remote(acc.at[:, pl.ds(0, 2), pl.ds(W, W), :], from_up.at[:, pl.ds(0, 2), :, :], y_send.at[CHUNKS], y_recv.at[CHUNKS], down)
-    )
-    for copy in y_copies:
-        copy.start()
-
+    corners = [(r[0], c[1]) for r in (up, down) for c in (west, east)]
+    links = Links(send, recv)
+    near, far = pl.ds(0, 2), pl.ds(2, 2)
+    ends = (pl.ds(0, 8), pl.ds(W - 8, 8))
+    side = lax.broadcasted_iota(jnp.int32, (W, LANE), 1) < LANE // 2
+
+    def sides_of(left, right):
+        turned = jnp.where(side, left, right).T
+        return jnp.concatenate([turned[:8, :], turned[LANE - 8 :, :]], axis=0)
+
+    def acc_sides(low):
+        rows = pl.ds(low * W, W)
+        for part in range(2):
+            for half in range(2):
+                strip[low, part, half, :, :] = sides_of(acc[part, 2 * half, rows, :], acc[part, 2 * half + 1, rows, :])
+
+    acc_sides(1)
+    greet([mate, beyond, *in_y, *in_col, *corners])
+
+    first_y = [links.start(strip.at[1], strip_up, down)]
+    for a, b in zip(ends, (pl.ds(W, 8), pl.ds(2 * W - 8, 8))):
+        first_y.append(links.start(acc.at[:, :, b, :], from_up.at[:, :, a, :], down))
     mine = pl.multiple_of(core * 512, 512)
     other = pl.multiple_of(512 - core * 512, 512)
-    a_copies = [remote(pacc.at[pl.ds(other, 512), :], p1, a_send.at[0], a_recv.at[0], mate)]
-    a_copies[0].start()
+    halves = links.start(pacc.at[pl.ds(other, 512), :], p1, mate)
+    high, low = pieces(SPILL), pieces(SPILL, W)
+    y_far = [links.copy(acc.at[:, far, b, :], from_up.at[:, far, a, :], down) for a, b in zip(high, low)]
+    y_near = [links.copy(acc.at[:, near, b, :], from_up.at[:, near, a, :], down) for a, b in zip(high, low)]
+    y_far[0].start()
+    acc_sides(0)
+    old_sides = [sides_of(ext_old[part, 0, pl.ds(0, W), :], ext_old[part, 1, pl.ds(0, W), :]) for part in range(2)]
+
+    def join(rows):
+        for part in range(2):
+            for t in range(2):
+                onward[part, t, rows, :] = acc[part, 2 + t, rows, :] + from_up[part, 2 + t, rows, :]
+
+    def step_rows(rows, to):
+        for part in range(2):
+            for t in range(2):
+                total = acc[part, t, rows, :] + from_up[part, t, rows, :] + from_west[part, t, rows, :]
+                frame[part, 1 + t, to, :] = ext_old[part, t, rows, :] + total * (1.0 / 16.0)
+
+    def over(bounds, k, size, work):
+        def one(i, _):
+            work(pl.multiple_of(i * size, size))
+            return 0
+
+        lax.fori_loop(bounds[k] // size, bounds[k + 1] // size, one, 0)
 
     x_copies = []
-    for k in range(CHUNKS):
-        y_copies[k].wait_recv()
-
-        def join(i, _):
-            o = pl.multiple_of(i * 16, 16)
-            for part in range(2):
-                for t in range(2):
-                    onward[part, t, pl.ds(k * CH + o, 16), :] = (
-                        acc[part, 2 + t, pl.ds(k * CH + o, 16), :] + from_up[part, 2 + t, pl.ds(k * CH + o, 16), :]
-                    )
-            return 0
-
-        lax.fori_loop(0, CH // 16, join, 0)
-        copy = remote(onward.at[:, :, chunk(k), :], from_west.at[:, :, chunk(k), :], x_send.at[k], x_recv.at[k], east)
-        copy.start()
-        x_copies.append(copy)
-
-    a_copies[0].wait_recv()
+
+    def pass_on(k):
+        y_far[k].wait_recv()
+        over(SPILL, k, 8, lambda o: join(pl.ds(o, 8)))
+        rows = pieces(SPILL)[k]
+        x_copies.append(links.start(onward.at[:, :, rows, :], from_west.at[:, :, rows, :], east))
+
+    y_far[0].wait_send()
+    y_far[1].start()
+    halves.wait_recv()
 
     def join_half(i, _):
         o = pl.multiple_of(i * 64, 64)
@@ -421,115 +476,84 @@
         return 0
 
     lax.fori_loop(0, 8, join_half, 0)
-    b_copies = []
-    for d in range(1, 4):
-        block = pl.multiple_of(lax.rem(y + d, 4) * LANE, LANE)
-        b_copies.append(remote(h1.at[pl.ds(block, LANE), :], p2.at[d - 1], b_send.at[d - 1], b_recv.at[d - 1], in_y[d - 1]))
-    for copy in b_copies:
-        copy.start()
-
-    for t in range(3):
-        for part in range(2):
-            frame[part, t, pl.ds(0, 8), :] = jnp.zeros((8, LANE), F32)
-            frame[part, t, pl.ds(FRAME - 8, 8), :] = jnp.zeros((8, LANE), F32)
-
-    def step_rows(k):
-        def add(i, _):
-            o = pl.multiple_of(k * CH + i * 16, 16)
-            rows = pl.ds(o, 16)
-            for part in range(2):
-                for t in range(2):
-                    total = acc[part, t, rows, :] + from_up[part, t, rows, :] + from_west[part, t, rows, :]
-                    frame[part, 1 + t, pl.ds(TOP + o, 16), :] = ext_old[part, t, rows, :] + total * (1.0 / 16.0)
-            return 0
-
-        lax.fori_loop(0, CH // 16, add, 0)
-
-    y_copies[CHUNKS].wait_recv()
-    for k in range(CHUNKS // 2):
-        x_copies[k].wait_recv()
-        step_rows(k)
-
-    for copy in b_copies:
+    for copy in first_y:
         copy.wait_recv()
-    here = pl.multiple_of(y * LANE, LANE)
-    h2[...] = h1[pl.ds(here, LANE), :] + p2[0] + p2[1] + p2[2]
-    c_copies = []
+    for a in ends:
+        join(a)
+    for part in range(2):
+        strip_on[part, :, :] = strip[0, part, 1, :, :] + strip_up[part, 1, :, :]
+    first_x = [links.start(strip_on, strip_west, east)]
+    for a in ends:
+        first_x.append(links.start(onward.at[:, :, a, :], from_west.at[:, :, a, :], east))
+
+    over_col = []
     for d in range(1, COLS):
-        block = pl.multiple_of(lax.rem(col + d, COLS) * 8, 8)
-        c_copies.append(remote(h2.at[pl.ds(block, 8), :], p3.at[d], c_send.at[d], c_recv.at[d], in_col[d - 1]))
-    for copy in c_copies:
-        copy.start()
-
-    for k in range(CHUNKS // 2, CHUNKS):
-        x_copies[k].wait_recv()
-        step_rows(k)
-
-    side = lax.broadcasted_iota(jnp.int32, (W, LANE), 1) < LANE // 2
+        block = pl.multiple_of(lax.rem(col + d, COLS) * 32, 32)
+        over_col.append(links.start(h1.at[pl.ds(block, 32), :], p2.at[d - 1], in_col[d - 1]))
+    y_far[1].wait_send()
+    y_far[2].start()
+    y_near[0].start()
+    pass_on(0)
+
+    for copy in first_x:
+        copy.wait_recv()
     for part in range(2):
-        ends = jnp.where(side, frame[part, 1, pl.ds(TOP, W), :], frame[part, 2, pl.ds(TOP, W), :]).T
-        rim_out[0, part, :, :] = ends[:8, :]
-        rim_out[1, part, :, :] = ends[LANE - 8 :, :]
+        total = strip[0, part, 0, :, :] + strip_up[part, 0, :, :] + strip_west[part, :, :]
+        strip_new[part, :, :] = old_sides[part] + total * (1.0 / 16.0)
+    step_rows(ends[0], pl.ds(TOP, 8))
+    step_rows(ends[1], pl.ds(TOP + W - 8, 8))
+    top_in, top_out = pl.ds(TOP - 8, 8), pl.ds(TOP, 8)
+    low_in, low_out = pl.ds(TOP + W, 8), pl.ds(TOP + W - 8, 8)
+    both = pl.ds(1, 2)
     rims = [
-        remote(rim_out.at[0], rim_in.at[0], rim_send.at[0], rim_recv.at[0], west),
-        remote(rim_out.at[1], rim_in.at[1], rim_send.at[1], rim_recv.at[1], east),
+        links.start(strip_new.at[:, pl.ds(0, 8), :], rim_in.at[0], west),
+        links.start(strip_new.at[:, pl.ds(8, 8), :], rim_in.at[1], east),
+        links.start(frame.at[:, both, top_out, :], frame.at[:, both, low_in, :], up),
+        links.start(frame.at[:, both, low_out, :], frame.at[:, both, top_in, :], down),
+        links.start(frame.at[:, 1, top_out, :], corner_in.at[0], corners[0]),
+        links.start(frame.at[:, 2, top_out, :], corner_in.at[1], corners[1]),
+        links.start(frame.at[:, 1, low_out, :], corner_in.at[2], corners[2]),
+        links.start(frame.at[:, 2, low_out, :], corner_in.at[3], corners[3]),
     ]
-    rims[0].start()
-    rims[1].start()
-
-    for copy in c_copies:
+    y_far[2].wait_send()
+    y_far[3].start()
+    y_near[1].start()
+    pass_on(1)
+    pass_on(2)
+    y_near[2].start()
+    for copy in over_col:
         copy.wait_recv()
-    own = pl.multiple_of(col * 8, 8)
-    total = h2[pl.ds(own, 8), :]
-    for d in range(1, COLS):
-        total = total + p3[d]
-    piece = pl.multiple_of(core * 512 + y * LANE + col * 8, 8)
-    flat[pl.ds(piece, 8), :] = flat_old[pl.ds(piece, 8), :] + total * (2.0 / math.sqrt(2048.0))
-    d_copies = []
-    for d in range(1, COLS):
-        d_copies.append(
-            remote(flat.at[pl.ds(piece, 8), :], flat.at[pl.ds(piece, 8), :], d_send.at[d], d_recv.at[d], in_col[d - 1])
-        )
-    for copy in d_copies:
-        copy.start()
-
-    rims[0].wait_recv()
-    rims[1].wait_recv()
+    here = pl.multiple_of(col * 32, 32)
+    total = h1[pl.ds(here, 32), :]
+    for d in range(COLS - 1):
+        total = total + p2[d]
+    h3[...] = total
+    over_y = [links.start(h3, p4.at[y], to) for to in in_y]
+    p4[y] = total
+
+    for copy in rims:
+        copy.wait_recv()
     blank = jnp.zeros((LANE - 16, W), F32)
+    lane8 = lax.broadcasted_iota(jnp.int32, (8, LANE), 1)
     for part in range(2):
         right_rim = jnp.where(col < COLS - 1, rim_in[0, part, :, :], 0.0)
         left_rim = jnp.where(col > 0, rim_in[1, part, :, :], 0.0)
         frame[part, 0, pl.ds(TOP, W), :] = jnp.concatenate([right_rim, blank, left_rim], axis=0).T
-    rows_out = [
-        remote(frame.at[:, :, pl.ds(TOP, 8), :], frame.at[:, :, pl.ds(TOP + W, 8), :], rim_send.at[2], rim_recv.at[2], up),
-        remote(frame.at[:, :, pl.ds(TOP + W - 8, 8), :], frame.at[:, :, pl.ds(TOP - 8, 8), :], rim_send.at[3], rim_recv.at[3], down),
-    ]
-    rows_out[0].start()
-    rows_out[1].start()
-
-    def gathered(first, count, send, recv, to):
-        return remote(flat.at[pl.ds(first, count), :], flat.at[pl.ds(first, count), :], send, recv, to)
-
-    for copy in d_copies:
-        copy.wait_recv()
-    quarter = pl.multiple_of(core * 512 + y * LANE, LANE)
-    for d in range(1, 4):
-        b_copies.append(gathered(quarter, LANE, b_send.at[2 + d], b_recv.at[2 + d], in_y[d - 1]))
-        b_copies[-1].start()
-
-    rows_out[0].wait_recv()
-    rows_out[1].wait_recv()
-    for part in range(2):
+        for on, rows, right, left in ((row > 0, top_in, 2, 3), (row < ROWS - 1, low_in, 0, 1)):
+            right_end = jnp.where(col < COLS - 1, corner_in[right, part, :, :], 0.0)
+            left_end = jnp.where(col > 0, corner_in[left, part, :, :], 0.0)
+            ends_in = jnp.where(lane8 < 8, right_end, jnp.where(lane8 >= LANE - 8, left_end, 0.0))
+            frame[part, 0, rows, :] = jnp.where(on, ends_in, 0.0)
+            for t in range(1, 3):
+                frame[part, t, rows, :] = jnp.where(on, frame[part, t, rows, :], 0.0)
         for t in range(3):
-            top = pl.ds(TOP - 8, 8)
-            low = pl.ds(TOP + W, 8)
-            frame[part, t, top, :] = jnp.where(row > 0, frame[part, t, top, :], 0.0)
-            frame[part, t, low, :] = jnp.where(row < ROWS - 1, frame[part, t, low, :], 0.0)
-
-    lane8 = lax.broadcasted_iota(jnp.int32, (8, LANE), 1)
-    lane32 = lax.broadcasted_iota(jnp.int32, (32, LANE), 1)
+            frame[part, t, pl.ds(0, 8), :] = jnp.zeros((8, LANE), F32)
+            frame[part, t, pl.ds(FRAME - 8, 8), :] = jnp.zeros((8, LANE), F32)
+
     west_on = (col > 0).astype(F32)
     east_on = (col < COLS - 1).astype(F32)
+    lane16 = lax.broadcasted_iota(jnp.int32, (16, LANE), 1)
+    lane32 = lax.broadcasted_iota(jnp.int32, (32, LANE), 1)
 
     def tap(ref):
         return lambda a, b: ref[a, step, b]
@@ -547,15 +571,9 @@
     first(TOP - 8, 8, lane8, (row > 0).astype(F32))
     first(TOP + W, 8, lane8, (row < ROWS - 1).astype(F32))
 
-    def first_rows(i, _):
-        first(pl.multiple_of(TOP + i * 32, 16), 32, lane32, None)
-        return 0
-
-    lax.fori_loop(0, W // 32, first_rows, 0)
-
-    def second(i):
-        o = pl.multiple_of(TOP + i * 32, 16)
-        at = pl.ds(pl.multiple_of(i * 32, 32), 32)
+    def second(o):
+        at = pl.ds(o, 32)
+        o = o + TOP
         parts = correlate_block(lambda t, a: real[t, pl.ds(a, 32), :], o, tap(kernel_second), range(1, 3), lane32)
         for t in range(2):
             new_re = real[1 + t, pl.ds(o, 32), :]
@@ -567,27 +585,53 @@
                 ext[0, t, at, :] = new_re
                 ext[1, t, at, :] = new_im
 
-    def second_rows(i, _):
-        second(i)
-        return 0
-
     if not last:
-        copies = halo_copies(lambda k: ext.at[:, pl.ds(0, 2), chunk(k), :], ext, h_send, h_recv, west, up)
-    for k in range(CHUNKS):
-        lax.fori_loop(k * CH // 32, (k + 1) * CH // 32, second_rows, 0)
+        copies = halo_copies(links, ext, LATER, west, up)
+
+    def settle(k):
+        y_near[k].wait_recv()
+        x_copies[k].wait_recv()
+        over(SPILL, k, 8, lambda o: step_rows(pl.ds(o, 8), pl.ds(o + TOP, 8)))
+        over(REAL, k, 16, lambda o: first(o + TOP, 16, lane16, None))
+        over(LATER, k, 32, second)
         if not last:
             copies[0][k].start()
             copies[1][k].start()
 
-    for copy in b_copies[3:]:
+    for copy in over_y:
         copy.wait_recv()
-    a_copies.append(gathered(mine, 512, a_send.at[1], a_recv.at[1], mate))
-    a_copies[1].start()
+    piece = pl.multiple_of(core * 512 + col * 32, 32)
+    total = p4[0] + p4[1] + p4[2] + p4[3]
+    flat[pl.ds(piece, 32), :] = flat_old[pl.ds(piece, 32), :] + total * (2.0 / math.sqrt(2048.0))
+
+    def gather(first, count, targets):
+        rows = pl.ds(first, count)
+        return [links.start(flat.at[rows, :], flat.at[rows, :], to) for to in targets]
+
+    back = gather(piece, 32, in_col)
+
+    settle(0)
+    pass_on(3)
+    y_near[3].start()
+    settle(1)
+    settle(2)
+    settle(3)
+    for copy in back:
+        copy.wait_recv()
+    back = gather(mine, 512, [mate])
     if not last:
-        halo_finish(copies)
-    a_copies[1].wait_recv()
-    for copy in [*y_copies, *x_copies, *a_copies, *b_copies, *c_copies, *d_copies, *rims, *rows_out]:
-        copy.wait_send()
+        for k in range(0, 2):
+            copies[0][k].wait_recv()
+            copies[2][k].start()
+    if not last:
+        for k in range(2, 4):
+            copies[0][k].wait_recv()
+            copies[2][k].start()
+    if not last:
+        for copy in [*copies[1], *copies[2]]:
+            copy.wait_recv()
+    back[0].wait_recv()
+    links.drain()
 
 
 def update_call(step, last, acc, ext, pacc, flat, kernel_first, kernel_second):
@@ -600,23 +644,22 @@
             pltpu.VMEM((2, 4, W, LANE), F32),
             pltpu.VMEM((2, 2, W, LANE), F32),
             pltpu.VMEM((2, 2, W, LANE), F32),
+            pltpu.VMEM((2, 2, 2, 16, W), F32),
+            pltpu.VMEM((2, 2, 16, W), F32),
+            pltpu.VMEM((2, 16, W), F32),
+            pltpu.VMEM((2, 16, W), F32),
+            pltpu.VMEM((2, 16, W), F32),
             pltpu.VMEM((2, 2, 8, W), F32),
-            pltpu.VMEM((2, 2, 8, W), F32),
+            pltpu.VMEM((4, 2, 8, LANE), F32),
             pltpu.VMEM((2, 3, FRAME, LANE), F32),
             pltpu.VMEM((3, FRAME, LANE), F32),
             pltpu.VMEM((512, LANE), F32),
             pltpu.VMEM((512, LANE), F32),
-            pltpu.VMEM((3, LANE, LANE), F32),
-            pltpu.VMEM((LANE, LANE), F32),
-            pltpu.VMEM((COLS, 8, LANE), F32),
-            DMA((CHUNKS + 1,)), DMA((CHUNKS + 1,)),
-            DMA((CHUNKS,)), DMA((CHUNKS,)),
-            DMA((4,)), DMA((4,)),
-            DMA((HALO_SEMS,)), DMA((HALO_SEMS,)),
-            DMA((2,)), DMA((2,)),
-            DMA((6,)), DMA((6,)),
-            DMA((COLS,)), DMA((COLS,)),
-            DMA((COLS,)), DMA((COLS,)),
+            pltpu.VMEM((COLS - 1, 32, LANE), F32),
+            pltpu.VMEM((32, LANE), F32),
+            pltpu.VMEM((4, 32, LANE), F32),
+            DMA((UPDATE_SEMS,)),
+            DMA((UPDATE_SEMS,)),
         ],
         compiler_params=pltpu.CompilerParams(
             collective_id=2 if last else 1, has_side_effects=True, vmem_limit_bytes=VLIM

time: 151 us -> 142 us (0.940)
  Pallas kernels: 143 us -> 134 us
    pallas_call x2, Pallas kernels: 89.4 us -> 80.1 us  [update_call(): pl.pallas_call(functools.partial(update_kernel, step, last), out_shape=(T...]
where the time goes in v3:
time: 142 us
  Pallas kernels  134 us (94%)
  local copies, waits for them, and re-layouts  6.22 us (4%)
    pallas_call x2, Pallas kernels, update_call(): pl.pallas_call(functools.partial(update_kernel, step, last), out_shape=(T...  80.1 us
    pallas_call x2, Pallas kernels, window_call(): pl.pallas_call(window_kernel, out_shape=(EXT, FLAT), in_specs=[SM, SM, VM...  32.2 us
    pallas_call x1, Pallas kernels, halo_call(): pl.pallas_call(halo_kernel, out_shape=(EXT, FLAT, jax.ShapeDtypeStruct(am...  22.2 us
    unnamed x21, local copies, waits for them, and re-layouts  5.39 us

profile of v3, /device:TPU:1, one launch (start us, length us, event | category | flops | bytes accessed | tf_op | source)
XLA Modules:
  0.0 142.1 jit_solution(6407224190099582239)
XLA Ops:
  0.6 0.0 copy-start.9
  1.3 0.0 copy-start
  1.3 1.6 %copy-done = bf16[16,256,256]{2,1,0:T(8,128)(2,1)S(1)} copy-done((bf16[16,256,256]{2,1,0:T(8,128)(2,1)S(1)}, bf16[16,256,256]{2,1,0:T(8,128)(2,1)}, u32[]{:S(2)}) %copy-start) | copy-done | bytes 2097176
  2.9 0.0 copy-start.4
  2.9 1.0 copy-done.4
  3.9 0.0 copy-start.5
  3.9 1.0 copy-done.5
  5.0 0.0 copy-start.6
  5.0 0.9 copy-done.6
  5.9 22.2 %first_halo.1 = (f32[2,4,512,128]{3,2,1,0:T(8,128)S(1)}, f32[1024,128]{1,0:T(8,128)S(1)}, bf16[16,256,256]{2,1,0:T(8,128)(2,1)S(1)}) custom-call(f32[2,256,256]{2,1,0:T(8,128)S(1)} %copy-done.4, f32[2,256,256]{2,1,0:T(8,128)S(1)} %copy-done.5, bf16[16,256,256]{2,1,0:T(8,128)(2,1)S(1)} %copy-done, bf16[256,256]{1,0:T(8,128)(2,1)S(1)} %copy-done.6), custom_call_target="tpu_custom_call" | custom-call | tf_op jit(solution)/shard_map/first_halo/pallas_call | solution.py:363
  28.1 0.0 copy-done.9
  28.1 0.0 copy-done.1
  28.1 0.0 copy-done.2
  28.1 0.0 copy-done.3
  28.1 0.0 copy-start.7
  28.1 0.0 copy-start.8
  28.1 15.9 %windows.2 = (f32[2,4,512,128]{3,2,1,0:T(8,128)S(1)}, f32[1024,128]{1,0:T(8,128)S(1)}) custom-call(s32[2,16]{1,0:T(2,128)S(1)} %bitcast.15, s32[1]{0:T(128)S(6)} %copy.18.live, f32[2,4,512,128]{3,2,1,0:T(8,128)S(1)} %get-tuple-element.13.ext.ext_old, f32[1024,128]{1,0:T(8,128)S(1)} %get-tuple-element.14.probe.flat_old, ...), custom_call_target="tpu_custom_call" | custom-call | tf_op jit(solution)/shard_map/windows/pallas_call | solution.py:215
  44.1 0.0 copy-done.7
  44.1 0.0 copy-done.8
  44.1 44.5 %update.1 = (f32[2,4,512,128]{3,2,1,0:T(8,128)S(1)}, f32[1024,128]{1,0:T(8,128)S(1)}) custom-call(f32[2,4,512,128]{3,2,1,0:T(8,128)S(1)} %get-tuple-element.16.acc, f32[2,4,512,128]{3,2,1,0:T(8,128)S(1)} %get-tuple-element.13.ext.ext_old, f32[1024,128]{1,0:T(8,128)S(1)} %get-tuple-element.17.pacc, f32[1024,128]{1,0:T(8,128)S(1)} %get-tuple-element.14.probe.flat_old, ...), custom_call_target="tpu_custom_call" | custom-call | tf_op jit(solution)/shard_map/update/pallas_call | solution.py:638
  88.6 16.3 %windows.3 = (f32[2,4,512,128]{3,2,1,0:T(8,128)S(1)}, f32[1024,128]{1,0:T(8,128)S(1)}) custom-call(s32[2,16]{1,0:T(2,128)S(1)} %bitcast.16, s32[1]{0:T(128)S(6)} %copy.18.live, f32[2,4,512,128]{3,2,1,0:T(8,128)S(1)} %get-tuple-element.18.ext.ext_old, f32[1024,128]{1,0:T(8,128)S(1)} %get-tuple-element.19.probe.flat_old, ...), custom_call_target="tpu_custom_call" | custom-call | tf_op jit(solution)/shard_map/windows/pallas_call | solution.py:215
  104.8 35.6 %last_update.1 = (f32[2,256,256]{2,1,0:T(8,128)S(1)}, f32[1024,128]{1,0:T(8,128)S(1)}) custom-call(f32[2,4,512,128]{3,2,1,0:T(8,128)S(1)} %get-tuple-element.20.acc, f32[2,4,512,128]{3,2,1,0:T(8,128)S(1)} %get-tuple-element.18.ext.ext_old, f32[1024,128]{1,0:T(8,128)S(1)} %get-tuple-element.21.pacc, f32[1024,128]{1,0:T(8,128)S(1)} %get-tuple-element.19.probe.flat_old, ...), custom_call_target="tpu_custom_call" | custom-call | tf_op jit(solution)/shard_map/last_update/pallas_call | solution.py:638
  140.5 0.8 copy.16
  141.3 0.8 copy.19
  (3 shorter events, 0.0 us)
Async XLA Ops:
  0.6 27.4 %copy-start.9 = (s32[16,2]{0,1:T(2,128)S(1)}, s32[16,2]{0,1:T(2,128)}, u32[]{:S(2)}) copy-start(s32[16,2]{0,1:T(2,128)} %param.13) | copy-start | bytes 388
  1.3 1.6 %copy-start = (bf16[16,256,256]{2,1,0:T(8,128)(2,1)S(1)}, bf16[16,256,256]{2,1,0:T(8,128)(2,1)}, u32[]{:S(2)}) copy-start(bf16[16,256,256]{2,1,0:T(8,128)(2,1)} %amps.1) | copy-start | bytes 6291460
  2.9 1.0 copy-start.4
  3.9 1.0 copy-start.5
  5.0 0.9 copy-start.6
  5.9 22.2 %copy-start.1 = (bf16[4,256,256]{2,1,0:T(8,128)(2,1)S(1)}, bf16[4,256,256]{2,1,0:T(8,128)(2,1)}, u32[]{:S(2)}) copy-start(bf16[4,256,256]{2,1,0:T(8,128)(2,1)} %constant.10.clone.tab) | copy-start | bytes 1572868
  5.9 22.2 %copy-start.2 = (bf16[512,512]{1,0:T(8,128)(2,1)S(1)}, bf16[512,512]{1,0:T(8,128)(2,1)}, u32[]{:S(2)}) copy-start(bf16[512,512]{1,0:T(8,128)(2,1)} %constant.9.clone.rtab) | copy-start | bytes 1572868
  5.9 22.2 %copy-start.3 = (bf16[512,512]{1,0:T(8,128)(2,1)S(1)}, bf16[512,512]{1,0:T(8,128)(2,1)}, u32[]{:S(2)}) copy-start(bf16[512,512]{1,0:T(8,128)(2,1)} %constant.8.clone.ltab) | copy-start | bytes 1572868
  28.1 16.0 %copy-start.7 = (f32[2,3,3]{2,0,1:T(2,128)S(1)}, f32[2,3,3]{2,0,1:T(2,128)}, u32[]{:S(2)}) copy-start(f32[2,3,3]{2,0,1:T(2,128)} %param.16) | copy-start | bytes 220
  28.1 16.0 %copy-start.8 = (f32[2,3,3]{2,0,1:T(2,128)S(1)}, f32[2,3,3]{2,0,1:T(2,128)}, u32[]{:S(2)}) copy-start(f32[2,3,3]{2,0,1:T(2,128)} %param.17) | copy-start | bytes 220

commit v4 on v3

--- a/solution.py
+++ b/solution.py
@@ -26,7 +26,7 @@
 BF16 = jnp.bfloat16
 VM = pl.BlockSpec(memory_space=pltpu.VMEM)
 SM = pl.BlockSpec(memory_space=pltpu.SMEM)
-ANY = pl.BlockSpec(memory_space=pl.ANY)
+HBM = pl.BlockSpec(memory_space=pltpu.HBM)
 EXT = jax.ShapeDtypeStruct((2, 4, 2 * W, LANE), F32)
 FLAT = jax.ShapeDtypeStruct((4 * W, LANE), F32)
 TILE = jax.ShapeDtypeStruct((2, W, W), F32)
@@ -49,9 +49,7 @@
         re, im = fr[odd::2, :H], fi[odd::2, :H]
         g = np.block([[re, -im], [im, re]])
         halves += [g, g.T]
-    sort = np.zeros((W, W), np.float32)
-    sort[np.arange(W), np.argsort(order)] = 1.0
-    return np.ascontiguousarray(left), np.ascontiguousarray(right), np.stack(halves), sort.astype(ml_dtypes.bfloat16)
+    return np.ascontiguousarray(left), np.ascontiguousarray(right), np.stack(halves)
 
 
 def dot(a, b):
@@ -144,33 +142,40 @@
     def unright(m, g, odd):
         cbuf[m, g, odd] = dot(bbuf[g, odd], tab[2 * odd])
 
-    def put(s, m, g, i):
-        r, q, sh = place_of(s)
-        keep = lane >= sh
+    def put(first, m, i):
         o = i * B
         rows = pl.ds(o, B)
-        terms = [[], []]
-        er, ei = cbuf[m, g, 0, rows, :H], cbuf[m, g, 0, rows, H:]
-        dr, di = cbuf[m, g, 1, rows, :H], cbuf[m, g, 1, rows, H:]
+        places = [place_of(first + g) for g in range(G)]
+        terms = [[[], []] for _ in range(G)]
         for t in range(2):
             cols = slice(t * LANE, (t + 1) * LANE)
             at_re = pl.ds(t * W + o, B)
             at_im = pl.ds((2 + t) * W + o, B)
             pr = probe[at_re, :]
             pi = probe[at_im, :]
-            cr, ci = (er - dr, ei - di) if t else (er + dr, ei + di)
-            wr = win[m, g, 0, rows, cols]
-            wi = win[m, g, 1, rows, cols]
-            pacc[at_re, :] += wr * cr + wi * ci
-            pacc[at_im, :] += wr * ci - wi * cr
-            terms[0].append(pltpu.roll(pr * cr + pi * ci, sh, 1))
-            terms[1].append(pltpu.roll(pr * ci - pi * cr, sh, 1))
-        at = pl.ds(r + o, B)
-        for part in range(2):
-            a, b = terms[part]
-            acc[part, q, at, :] += jnp.where(keep, a, 0.0)
-            acc[part, q + 1, at, :] += jnp.where(keep, b, a)
-            acc[part, q + 2, at, :] += jnp.where(keep, 0.0, b)
+            sum_re, sum_im = pacc[at_re, :], pacc[at_im, :]
+            for g in range(G):
+                sh = places[g][2]
+                er, ei = cbuf[m, g, 0, rows, :H], cbuf[m, g, 0, rows, H:]
+                dr, di = cbuf[m, g, 1, rows, :H], cbuf[m, g, 1, rows, H:]
+                cr, ci = (er - dr, ei - di) if t else (er + dr, ei + di)
+                wr = win[m, g, 0, rows, cols]
+                wi = win[m, g, 1, rows, cols]
+                sum_re += wr * cr + wi * ci
+                sum_im += wr * ci - wi * cr
+                terms[g][0].append(pltpu.roll(pr * cr + pi * ci, sh, 1))
+                terms[g][1].append(pltpu.roll(pr * ci - pi * cr, sh, 1))
+            pacc[at_re, :] = sum_re
+            pacc[at_im, :] = sum_im
+        for g in range(G):
+            r, q, sh = places[g]
+            keep = lane >= sh
+            at = pl.ds(r + o, B)
+            for part in range(2):
+                a, b = terms[g][part]
+                acc[part, q, at, :] += jnp.where(keep, a, 0.0)
+                acc[part, q + 1, at, :] += jnp.where(keep, b, a)
+                acc[part, q + 2, at, :] += jnp.where(keep, 0.0, b)
 
     def stage(p, m):
         before = jnp.maximum(p - 1, 0)
@@ -185,9 +190,9 @@
         for g in range(G):
             main += [lambda g=g, h=h: unright(m, g, h) for h in range(2)]
         side = []
-        for g in range(G):
-            for i in range(W // B):
-                side += [lambda g=g, i=i: put(before * G + g, 1 - m, g, i), lambda g=g, i=i: form(after * G + g, 1 - m, g, i)]
+        for i in range(W // B):
+            side.append(lambda i=i: put(before * G, 1 - m, i))
+            side += [lambda g=g, i=i: form(after * G + g, 1 - m, g, i) for g in range(G)]
         done = 0
         for n, work in enumerate(main):
             work()
@@ -206,9 +211,8 @@
         return 0
 
     lax.fori_loop(0, groups // 2, step, 0)
-    for g in range(G):
-        for i in range(W // B):
-            put(slots - G + g, 1, g, i)
+    for i in range(W // B):
+        put(slots - G, 1, i)
 
 
 def window_call(places, live, ext, probe, amps, ltab, rtab, tab):
@@ -246,10 +250,11 @@
     return row, col, up, down, west, east
 
 
-def greet(targets):
+def greet(targets, meanwhile=lambda: None):
     barrier = pltpu.get_barrier_semaphore()
     for target in targets:
         pl.semaphore_signal(barrier, inc=1, device_id=target, device_id_type=MESH)
+    meanwhile()
     pl.semaphore_wait(barrier, len(targets))
 
 
@@ -300,7 +305,7 @@
 UPDATE_SEMS = 96
 
 
-def halo_kernel(obj, probe, amps, sort, ext, flat, amps_out, amps_in, send, recv, local, amp_sem):
+def halo_kernel(obj, probe, amps, ext, flat, amps_out, amps_in, sort, send, recv, local, amp_sem):
     row, col, up, down, west, east = where_am_i()
     slots = amps.shape[0]
     inward = [
@@ -330,6 +335,9 @@
         to_west[k].start()
     to_up[0].start()
     to_up[1].start()
+    at = lax.broadcasted_iota(jnp.int32, (W, W), 0)
+    to = lax.broadcasted_iota(jnp.int32, (W, W), 1)
+    sort[...] = jnp.where(at == jnp.where(to < H, 2 * to, 2 * to + 1 - W), 1.0, 0.0).astype(BF16)
     fill.wait()
 
     def reorder(s):
@@ -359,14 +367,15 @@
     links.drain()
 
 
-def halo_call(obj, probe, amps, sort):
+def halo_call(obj, probe, amps):
     return pl.pallas_call(
         halo_kernel,
         out_shape=(EXT, FLAT, jax.ShapeDtypeStruct(amps.shape, BF16)),
-        in_specs=[ANY, ANY, ANY, VM],
+        in_specs=[HBM, HBM, HBM],
         out_specs=(VM, VM, VM),
         scratch_shapes=[
             pltpu.VMEM(amps.shape, BF16),
+            pltpu.VMEM((W, W), BF16),
             DMA((HALO_SEMS,)),
             DMA((HALO_SEMS,)),
             DMA((6,)),
@@ -374,7 +383,7 @@
         ],
         compiler_params=pltpu.CompilerParams(collective_id=0, has_side_effects=True, vmem_limit_bytes=VLIM),
         name="first_halo",
-    )(obj, probe, amps, sort)
+    )(*(pltpu.with_memory_space_constraint(v, pltpu.HBM) for v in (obj, probe, amps)))
 
 
 TOP = 16
@@ -424,8 +433,7 @@
             for half in range(2):
                 strip[low, part, half, :, :] = sides_of(acc[part, 2 * half, rows, :], acc[part, 2 * half + 1, rows, :])
 
-    acc_sides(1)
-    greet([mate, beyond, *in_y, *in_col, *corners])
+    greet([mate, beyond, *in_y, *in_col, *corners], lambda: acc_sides(1))
 
     first_y = [links.start(strip.at[1], strip_up, down)]
     for a, b in zip(ends, (pl.ds(W, 8), pl.ds(2 * W - 8, 8))):
@@ -437,6 +445,7 @@
     y_far = [links.copy(acc.at[:, far, b, :], from_up.at[:, far, a, :], down) for a, b in zip(high, low)]
     y_near = [links.copy(acc.at[:, near, b, :], from_up.at[:, near, a, :], down) for a, b in zip(high, low)]
     y_far[0].start()
+    y_far[1].start()
     acc_sides(0)
     old_sides = [sides_of(ext_old[part, 0, pl.ds(0, W), :], ext_old[part, 1, pl.ds(0, W), :]) for part in range(2)]
 
@@ -466,8 +475,6 @@
         rows = pieces(SPILL)[k]
         x_copies.append(links.start(onward.at[:, :, rows, :], from_west.at[:, :, rows, :], east))
 
-    y_far[0].wait_send()
-    y_far[1].start()
     halves.wait_recv()
 
     def join_half(i, _):
@@ -669,12 +676,12 @@
 
 
 def body(object_field, probe, positions, amplitudes, live, kernel_first, kernel_second):
-    ltab, rtab, tab, sort = (jnp.asarray(table) for table in dft_tables())
+    ltab, rtab, tab = (jnp.asarray(table) for table in dft_tables())
     places = positions.T
     kernel_first = kernel_first.transpose(1, 0, 2)
     kernel_second = kernel_second.transpose(1, 0, 2)
     iters = kernel_first.shape[1]
-    ext, flat, amps = halo_call(object_field, probe, amplitudes, sort)
+    ext, flat, amps = halo_call(object_field, probe, amplitudes)
     for step in range(iters):
         acc, pacc = window_call(places, live, ext, flat, amps, ltab, rtab, tab)
         ext, flat = update_call(step, step == iters - 1, acc, ext, pacc, flat, kernel_first, kernel_second)

time: 142 us -> 135 us (0.951)
  local copies, waits for them, and re-layouts: 6.22 us -> 1.66 us
  Pallas kernels: 134 us -> 131 us
    unnamed x21 -> x13, local copies, waits for them, and re-layouts: 5.39 us -> 0.83 us
    pallas_call x2, Pallas kernels: 80.1 us -> 77.4 us  [update_call(): pl.pallas_call(functools.partial(update_kernel, step, last), out_shape=(T...]
where the time goes in v4:
time: 135 us; the launch traced here: 134 us
  Pallas kernels  131 us (97%)
  local copies, waits for them, and re-layouts  1.66 us (1%)
  between operations  1.52 us (1%)
    pallas_call x2, Pallas kernels, update_call(): pl.pallas_call(functools.partial(update_kernel, step, last), out_shape=(T...  77.4 us
    pallas_call x2, Pallas kernels, window_call(): pl.pallas_call(window_kernel, out_shape=(EXT, FLAT), in_specs=[SM, SM, VM...  31.8 us
    pallas_call x1, Pallas kernels, halo_call(): pl.pallas_call(halo_kernel, out_shape=(EXT, FLAT, jax.ShapeDtypeStruct(am...  22.1 us

profile of v4, /device:TPU:1, one launch (start us, length us, event | category | flops | bytes accessed | tf_op | source)
XLA Modules:
  0.0 134.4 jit_solution(16616751515744885431)
XLA Ops:
  0.6 0.0 copy-start
  0.6 0.0 copy-start.1
  0.7 0.0 copy-start.2
  0.7 0.0 copy-start.5
  1.4 22.1 %first_halo.1 = (f32[2,4,512,128]{3,2,1,0:T(8,128)S(1)}, f32[1024,128]{1,0:T(8,128)S(1)}, bf16[16,256,256]{2,1,0:T(8,128)(2,1)S(1)}) custom-call(f32[2,256,256]{2,1,0:T(8,128)} %obj.1, f32[2,256,256]{2,1,0:T(8,128)} %probe.1, bf16[16,256,256]{2,1,0:T(8,128)(2,1)} %amps.1), custom_call_target="tpu_custom_call" | custom-call | tf_op jit(solution)/shard_map/first_halo/pallas_call | solution.py:371
  23.5 0.0 copy-done
  23.5 0.0 copy-done.1
  23.6 0.0 copy-done.2
  23.6 0.0 copy-done.5
  23.6 0.0 copy-start.3
  23.6 0.0 copy-start.4
  23.6 15.8 %windows.2 = (f32[2,4,512,128]{3,2,1,0:T(8,128)S(1)}, f32[1024,128]{1,0:T(8,128)S(1)}) custom-call(s32[2,16]{1,0:T(2,128)S(1)} %bitcast.15, s32[1]{0:T(128)S(6)} %copy.17.live, f32[2,4,512,128]{3,2,1,0:T(8,128)S(1)} %get-tuple-element.13.ext.ext_old, f32[1024,128]{1,0:T(8,128)S(1)} %get-tuple-element.14.probe.flat_old, ...), custom_call_target="tpu_custom_call" | custom-call | tf_op jit(solution)/shard_map/windows/pallas_call | solution.py:219
  39.4 0.0 copy-done.3
  39.4 0.0 copy-done.4
  39.4 43.4 %update.1 = (f32[2,4,512,128]{3,2,1,0:T(8,128)S(1)}, f32[1024,128]{1,0:T(8,128)S(1)}) custom-call(f32[2,4,512,128]{3,2,1,0:T(8,128)S(1)} %get-tuple-element.16.acc, f32[2,4,512,128]{3,2,1,0:T(8,128)S(1)} %get-tuple-element.13.ext.ext_old, f32[1024,128]{1,0:T(8,128)S(1)} %get-tuple-element.17.pacc, f32[1024,128]{1,0:T(8,128)S(1)} %get-tuple-element.14.probe.flat_old, ...), custom_call_target="tpu_custom_call" | custom-call | tf_op jit(solution)/shard_map/update/pallas_call | solution.py:645
  82.9 15.9 %windows.3 = (f32[2,4,512,128]{3,2,1,0:T(8,128)S(1)}, f32[1024,128]{1,0:T(8,128)S(1)}) custom-call(s32[2,16]{1,0:T(2,128)S(1)} %bitcast.16, s32[1]{0:T(128)S(6)} %copy.17.live, f32[2,4,512,128]{3,2,1,0:T(8,128)S(1)} %get-tuple-element.18.ext.ext_old, f32[1024,128]{1,0:T(8,128)S(1)} %get-tuple-element.19.probe.flat_old, ...), custom_call_target="tpu_custom_call" | custom-call | tf_op jit(solution)/shard_map/windows/pallas_call | solution.py:219
  98.8 33.9 %last_update.1 = (f32[2,256,256]{2,1,0:T(8,128)S(1)}, f32[1024,128]{1,0:T(8,128)S(1)}) custom-call(f32[2,4,512,128]{3,2,1,0:T(8,128)S(1)} %get-tuple-element.20.acc, f32[2,4,512,128]{3,2,1,0:T(8,128)S(1)} %get-tuple-element.18.ext.ext_old, f32[1024,128]{1,0:T(8,128)S(1)} %get-tuple-element.21.pacc, f32[1024,128]{1,0:T(8,128)S(1)} %get-tuple-element.19.probe.flat_old, ...), custom_call_target="tpu_custom_call" | custom-call | tf_op jit(solution)/shard_map/last_update/pallas_call | solution.py:645
  132.8 0.8 copy.15
  133.6 0.8 copy.18
Async XLA Ops:
  0.6 22.9 %copy-start = (bf16[4,256,256]{2,1,0:T(8,128)(2,1)S(1)}, bf16[4,256,256]{2,1,0:T(8,128)(2,1)}, u32[]{:S(2)}) copy-start(bf16[4,256,256]{2,1,0:T(8,128)(2,1)} %constant.8.clone.tab) | copy-start | bytes 1572868
  0.6 22.9 %copy-start.1 = (bf16[512,512]{1,0:T(8,128)(2,1)S(1)}, bf16[512,512]{1,0:T(8,128)(2,1)}, u32[]{:S(2)}) copy-start(bf16[512,512]{1,0:T(8,128)(2,1)} %constant.7.clone.rtab) | copy-start | bytes 1572868
  0.7 22.9 %copy-start.2 = (bf16[512,512]{1,0:T(8,128)(2,1)S(1)}, bf16[512,512]{1,0:T(8,128)(2,1)}, u32[]{:S(2)}) copy-start(bf16[512,512]{1,0:T(8,128)(2,1)} %constant.6.clone.ltab) | copy-start | bytes 1572868
  0.7 22.9 %copy-start.5 = (s32[16,2]{0,1:T(2,128)S(1)}, s32[16,2]{0,1:T(2,128)}, u32[]{:S(2)}) copy-start(s32[16,2]{0,1:T(2,128)} %param.12) | copy-start | bytes 388
  23.6 15.9 %copy-start.3 = (f32[2,3,3]{2,0,1:T(2,128)S(1)}, f32[2,3,3]{2,0,1:T(2,128)}, u32[]{:S(2)}) copy-start(f32[2,3,3]{2,0,1:T(2,128)} %param.15) | copy-start | bytes 220
  23.6 15.9 %copy-start.4 = (f32[2,3,3]{2,0,1:T(2,128)S(1)}, f32[2,3,3]{2,0,1:T(2,128)}, u32[]{:S(2)}) copy-start(f32[2,3,3]{2,0,1:T(2,128)} %param.16) | copy-start | bytes 220

commit v5 on v4

--- a/solution.py
+++ b/solution.py
@@ -75,15 +75,6 @@
 
     lax.fori_loop(0, 16, zero_probe, 0)
 
-    def zero_last(i, _):
-        rows = pl.ds(pl.multiple_of(i * 16, 16), 16)
-        for g in range(G):
-            for part in range(2):
-                win[1, g, part, rows, :] = jnp.zeros((16, W), F32)
-                cbuf[1, g, part, rows, :] = jnp.zeros((16, W), F32)
-        return 0
-
-    lax.fori_loop(0, 16, zero_last, 0)
     B = 16
     lane = lax.broadcasted_iota(jnp.int32, (B, LANE), 1)
 
@@ -177,9 +168,8 @@
                 acc[part, q + 1, at, :] += jnp.where(keep, b, a)
                 acc[part, q + 2, at, :] += jnp.where(keep, 0.0, b)
 
-    def stage(p, m):
-        before = jnp.maximum(p - 1, 0)
-        after = jnp.minimum(p + 1, groups - 1)
+    def stage(p, m, place=True, prepare=True):
+        before, after = p - 1, p + 1
         main = []
         for g in range(G):
             main += [lambda g=g, h=h: left(m, g, h) for h in range(2)]
@@ -191,8 +181,10 @@
             main += [lambda g=g, h=h: unright(m, g, h) for h in range(2)]
         side = []
         for i in range(W // B):
-            side.append(lambda i=i: put(before * G, 1 - m, i))
-            side += [lambda g=g, i=i: form(after * G + g, 1 - m, g, i) for g in range(G)]
+            if place:
+                side.append(lambda i=i: put(before * G, 1 - m, i))
+            if prepare:
+                side += [lambda g=g, i=i: form(after * G + g, 1 - m, g, i) for g in range(G)]
         done = 0
         for n, work in enumerate(main):
             work()
@@ -206,11 +198,13 @@
             form(g, 0, g, i)
 
     def step(p, _):
-        stage(2 * p, 0)
         stage(2 * p + 1, 1)
+        stage(2 * p + 2, 0)
         return 0
 
-    lax.fori_loop(0, groups // 2, step, 0)
+    stage(0, 0, place=False)
+    lax.fori_loop(0, groups // 2 - 1, step, 0)
+    stage(groups - 1, 1, prepare=False)
     for i in range(W // B):
         put(slots - G, 1, i)
 
@@ -475,14 +469,6 @@
         rows = pieces(SPILL)[k]
         x_copies.append(links.start(onward.at[:, :, rows, :], from_west.at[:, :, rows, :], east))
 
-    halves.wait_recv()
-
-    def join_half(i, _):
-        o = pl.multiple_of(i * 64, 64)
-        h1[pl.ds(o, 64), :] = pacc[pl.ds(mine + o, 64), :] + p1[pl.ds(o, 64), :]
-        return 0
-
-    lax.fori_loop(0, 8, join_half, 0)
     for copy in first_y:
         copy.wait_recv()
     for a in ends:
@@ -493,6 +479,14 @@
     for a in ends:
         first_x.append(links.start(onward.at[:, :, a, :], from_west.at[:, :, a, :], east))
 
+    halves.wait_recv()
+
+    def join_half(i, _):
+        o = pl.multiple_of(i * 64, 64)
+        h1[pl.ds(o, 64), :] = pacc[pl.ds(mine + o, 64), :] + p1[pl.ds(o, 64), :]
+        return 0
+
+    lax.fori_loop(0, 8, join_half, 0)
     over_col = []
     for d in range(1, COLS):
         block = pl.multiple_of(lax.rem(col + d, COLS) * 32, 32)
@@ -622,10 +616,10 @@
     y_near[3].start()
     settle(1)
     settle(2)
-    settle(3)
     for copy in back:
         copy.wait_recv()
     back = gather(mine, 512, [mate])
+    settle(3)
     if not last:
         for k in range(0, 2):
             copies[0][k].wait_recv()

time: 135 us -> 131 us (0.970)
  Pallas kernels: 131 us -> 128 us
    pallas_call x2, Pallas kernels: 31.8 us -> 29.8 us  [window_call(): pl.pallas_call(window_kernel, out_shape=(EXT, FLAT), in_specs=[SM, SM, VM...]
where the time goes in v5:
time: 131 us
  Pallas kernels  128 us (98%)
  local copies, waits for them, and re-layouts  1.66 us (1%)
  between operations  1.52 us (1%)
    pallas_call x2, Pallas kernels, update_call(): pl.pallas_call(functools.partial(update_kernel, step, last), out_shape=(T...  76.2 us
    pallas_call x2, Pallas kernels, window_call(): pl.pallas_call(window_kernel, out_shape=(EXT, FLAT), in_specs=[SM, SM, VM...  29.8 us
    pallas_call x1, Pallas kernels, halo_call(): pl.pallas_call(halo_kernel, out_shape=(EXT, FLAT, jax.ShapeDtypeStruct(am...  22.1 us

profile of v5, /device:TPU:1, one launch (start us, length us, event | category | flops | bytes accessed | tf_op | source)
XLA Modules:
  0.0 131.3 jit_solution(11528309612368508867)
XLA Ops:
  0.6 0.0 copy-start
  0.6 0.0 copy-start.1
  0.7 0.0 copy-start.2
  0.7 0.0 copy-start.5
  1.4 22.1 %first_halo.1 = (f32[2,4,512,128]{3,2,1,0:T(8,128)S(1)}, f32[1024,128]{1,0:T(8,128)S(1)}, bf16[16,256,256]{2,1,0:T(8,128)(2,1)S(1)}) custom-call(f32[2,256,256]{2,1,0:T(8,128)} %obj.1, f32[2,256,256]{2,1,0:T(8,128)} %probe.1, bf16[16,256,256]{2,1,0:T(8,128)(2,1)} %amps.1), custom_call_target="tpu_custom_call" | custom-call | tf_op jit(solution)/shard_map/first_halo/pallas_call | solution.py:365
  23.5 0.0 copy-done
  23.5 0.0 copy-done.1
  23.6 0.0 copy-done.2
  23.6 0.0 copy-done.5
  23.6 0.0 copy-start.3
  23.6 0.0 copy-start.4
  23.6 14.8 %windows.2 = (f32[2,4,512,128]{3,2,1,0:T(8,128)S(1)}, f32[1024,128]{1,0:T(8,128)S(1)}) custom-call(s32[2,16]{1,0:T(2,128)S(1)} %bitcast.15, s32[1]{0:T(128)S(6)} %copy.17.live, f32[2,4,512,128]{3,2,1,0:T(8,128)S(1)} %get-tuple-element.13.ext.ext_old, f32[1024,128]{1,0:T(8,128)S(1)} %get-tuple-element.14.probe.flat_old, ...), custom_call_target="tpu_custom_call" | custom-call | tf_op jit(solution)/shard_map/windows/pallas_call | solution.py:213
  38.4 0.0 copy-done.3
  38.4 0.0 copy-done.4
  38.5 43.4 %update.1 = (f32[2,4,512,128]{3,2,1,0:T(8,128)S(1)}, f32[1024,128]{1,0:T(8,128)S(1)}) custom-call(f32[2,4,512,128]{3,2,1,0:T(8,128)S(1)} %get-tuple-element.16.acc, f32[2,4,512,128]{3,2,1,0:T(8,128)S(1)} %get-tuple-element.13.ext.ext_old, f32[1024,128]{1,0:T(8,128)S(1)} %get-tuple-element.17.pacc, f32[1024,128]{1,0:T(8,128)S(1)} %get-tuple-element.14.probe.flat_old, ...), custom_call_target="tpu_custom_call" | custom-call | tf_op jit(solution)/shard_map/update/pallas_call | solution.py:639
  81.8 15.0 %windows.3 = (f32[2,4,512,128]{3,2,1,0:T(8,128)S(1)}, f32[1024,128]{1,0:T(8,128)S(1)}) custom-call(s32[2,16]{1,0:T(2,128)S(1)} %bitcast.16, s32[1]{0:T(128)S(6)} %copy.17.live, f32[2,4,512,128]{3,2,1,0:T(8,128)S(1)} %get-tuple-element.18.ext.ext_old, f32[1024,128]{1,0:T(8,128)S(1)} %get-tuple-element.19.probe.flat_old, ...), custom_call_target="tpu_custom_call" | custom-call | tf_op jit(solution)/shard_map/windows/pallas_call | solution.py:213
  96.8 32.9 %last_update.1 = (f32[2,256,256]{2,1,0:T(8,128)S(1)}, f32[1024,128]{1,0:T(8,128)S(1)}) custom-call(f32[2,4,512,128]{3,2,1,0:T(8,128)S(1)} %get-tuple-element.20.acc, f32[2,4,512,128]{3,2,1,0:T(8,128)S(1)} %get-tuple-element.18.ext.ext_old, f32[1024,128]{1,0:T(8,128)S(1)} %get-tuple-element.21.pacc, f32[1024,128]{1,0:T(8,128)S(1)} %get-tuple-element.19.probe.flat_old, ...), custom_call_target="tpu_custom_call" | custom-call | tf_op jit(solution)/shard_map/last_update/pallas_call | solution.py:639
  129.7 0.8 copy.15
  130.5 0.8 copy.18
Async XLA Ops:
  0.6 22.9 %copy-start = (bf16[4,256,256]{2,1,0:T(8,128)(2,1)S(1)}, bf16[4,256,256]{2,1,0:T(8,128)(2,1)}, u32[]{:S(2)}) copy-start(bf16[4,256,256]{2,1,0:T(8,128)(2,1)} %constant.8.clone.tab) | copy-start | bytes 1572868
  0.6 22.9 %copy-start.1 = (bf16[512,512]{1,0:T(8,128)(2,1)S(1)}, bf16[512,512]{1,0:T(8,128)(2,1)}, u32[]{:S(2)}) copy-start(bf16[512,512]{1,0:T(8,128)(2,1)} %constant.7.clone.rtab) | copy-start | bytes 1572868
  0.7 22.9 %copy-start.2 = (bf16[512,512]{1,0:T(8,128)(2,1)S(1)}, bf16[512,512]{1,0:T(8,128)(2,1)}, u32[]{:S(2)}) copy-start(bf16[512,512]{1,0:T(8,128)(2,1)} %constant.6.clone.ltab) | copy-start | bytes 1572868
  0.7 22.9 %copy-start.5 = (s32[16,2]{0,1:T(2,128)S(1)}, s32[16,2]{0,1:T(2,128)}, u32[]{:S(2)}) copy-start(s32[16,2]{0,1:T(2,128)} %param.12) | copy-start | bytes 388
  23.6 14.9 %copy-start.3 = (f32[2,3,3]{2,0,1:T(2,128)S(1)}, f32[2,3,3]{2,0,1:T(2,128)}, u32[]{:S(2)}) copy-start(f32[2,3,3]{2,0,1:T(2,128)} %param.15) | copy-start | bytes 220
  23.6 14.9 %copy-start.4 = (f32[2,3,3]{2,0,1:T(2,128)S(1)}, f32[2,3,3]{2,0,1:T(2,128)}, u32[]{:S(2)}) copy-start(f32[2,3,3]{2,0,1:T(2,128)} %param.16) | copy-start | bytes 220

commit v6 on v5

--- a/solution.py
+++ b/solution.py
@@ -669,6 +669,34 @@
     )(acc, ext, pacc, flat, kernel_first, kernel_second)
 
 
+def deliver_kernel(tile, flat, obj_out, probe_out, sems):
+    copies = [pltpu.make_async_copy(tile, obj_out, sems.at[4])]
+    for part in range(2):
+        for t in range(2):
+            n = part * 2 + t
+            copies.append(
+                pltpu.make_async_copy(
+                    flat.at[pl.ds(n * W, W), :], probe_out.at[part, :, pl.ds(t * LANE, LANE)], sems.at[n]
+                )
+            )
+    for copy in copies:
+        copy.start()
+    for copy in copies:
+        copy.wait()
+
+
+def deliver_call(tile, flat):
+    return pl.pallas_call(
+        deliver_kernel,
+        out_shape=(TILE, TILE),
+        in_specs=[VM, VM],
+        out_specs=(HBM, HBM),
+        scratch_shapes=[DMA((5,))],
+        compiler_params=pltpu.CompilerParams(vmem_limit_bytes=VLIM),
+        name="deliver",
+    )(tile, flat)
+
+
 def body(object_field, probe, positions, amplitudes, live, kernel_first, kernel_second):
     ltab, rtab, tab = (jnp.asarray(table) for table in dft_tables())
     places = positions.T
@@ -679,7 +707,7 @@
     for step in range(iters):
         acc, pacc = window_call(places, live, ext, flat, amps, ltab, rtab, tab)
         ext, flat = update_call(step, step == iters - 1, acc, ext, pacc, flat, kernel_first, kernel_second)
-    return ext, flat.reshape(2, 2, W, LANE).transpose(0, 2, 1, 3).reshape(2, W, W)
+    return deliver_call(ext, flat)
 
 
 def solution(mesh):

time: 131 us -> 131 us (level)
  local copies, waits for them, and re-layouts: 1.66 us -> 0.04 us
where the time goes in v6:
time: 131 us
  Pallas kernels  129 us (98%)
  between operations  1.68 us (1%)
    pallas_call x2, Pallas kernels, update_call(): pl.pallas_call(functools.partial(update_kernel, step, last), out_shape=(T...  76.3 us
    pallas_call x2, Pallas kernels, window_call(): pl.pallas_call(window_kernel, out_shape=(EXT, FLAT), in_specs=[SM, SM, VM...  29.8 us
    pallas_call x1, Pallas kernels, halo_call(): pl.pallas_call(halo_kernel, out_shape=(EXT, FLAT, jax.ShapeDtypeStruct(am...  22.1 us

profile of v6, /device:TPU:1, one launch (start us, length us, event | category | flops | bytes accessed | tf_op | source)
XLA Modules:
  0.0 130.9 jit_solution(11270702584237518028)
XLA Ops:
  0.6 0.0 copy-start
  0.6 0.0 copy-start.1
  0.7 0.0 copy-start.2
  0.7 0.0 copy-start.5
  1.4 22.1 %first_halo.1 = (f32[2,4,512,128]{3,2,1,0:T(8,128)S(1)}, f32[1024,128]{1,0:T(8,128)S(1)}, bf16[16,256,256]{2,1,0:T(8,128)(2,1)S(1)}) custom-call(f32[2,256,256]{2,1,0:T(8,128)} %obj.1, f32[2,256,256]{2,1,0:T(8,128)} %probe.1, bf16[16,256,256]{2,1,0:T(8,128)(2,1)} %amps.1), custom_call_target="tpu_custom_call" | custom-call | tf_op jit(solution)/shard_map/first_halo/pallas_call | solution.py:365
  23.5 0.0 copy-done
  23.5 0.0 copy-done.1
  23.6 0.0 copy-done.2
  23.6 0.0 copy-done.5
  23.6 0.0 copy-start.3
  23.6 0.0 copy-start.4
  23.6 14.8 %windows.2 = (f32[2,4,512,128]{3,2,1,0:T(8,128)S(1)}, f32[1024,128]{1,0:T(8,128)S(1)}) custom-call(s32[2,16]{1,0:T(2,128)S(1)} %bitcast.7, s32[1]{0:T(128)S(6)} %copy.12.live, f32[2,4,512,128]{3,2,1,0:T(8,128)S(1)} %get-tuple-element.13.ext.ext_old, f32[1024,128]{1,0:T(8,128)S(1)} %get-tuple-element.14.probe.flat_old, ...), custom_call_target="tpu_custom_call" | custom-call | tf_op jit(solution)/shard_map/windows/pallas_call | solution.py:213
  38.4 0.0 copy-done.3
  38.4 0.0 copy-done.4
  38.4 43.4 %update.1 = (f32[2,4,512,128]{3,2,1,0:T(8,128)S(1)}, f32[1024,128]{1,0:T(8,128)S(1)}) custom-call(f32[2,4,512,128]{3,2,1,0:T(8,128)S(1)} %get-tuple-element.16.acc, f32[2,4,512,128]{3,2,1,0:T(8,128)S(1)} %get-tuple-element.13.ext.ext_old, f32[1024,128]{1,0:T(8,128)S(1)} %get-tuple-element.17.pacc, f32[1024,128]{1,0:T(8,128)S(1)} %get-tuple-element.14.probe.flat_old, ...), custom_call_target="tpu_custom_call" | custom-call | tf_op jit(solution)/shard_map/update/pallas_call | solution.py:639
  81.9 15.0 %windows.3 = (f32[2,4,512,128]{3,2,1,0:T(8,128)S(1)}, f32[1024,128]{1,0:T(8,128)S(1)}) custom-call(s32[2,16]{1,0:T(2,128)S(1)} %bitcast.8, s32[1]{0:T(128)S(6)} %copy.12.live, f32[2,4,512,128]{3,2,1,0:T(8,128)S(1)} %get-tuple-element.18.ext.ext_old, f32[1024,128]{1,0:T(8,128)S(1)} %get-tuple-element.19.probe.flat_old, ...), custom_call_target="tpu_custom_call" | custom-call | tf_op jit(solution)/shard_map/windows/pallas_call | solution.py:213
  96.8 32.9 %last_update.1 = (f32[2,256,256]{2,1,0:T(8,128)S(1)}, f32[1024,128]{1,0:T(8,128)S(1)}) custom-call(f32[2,4,512,128]{3,2,1,0:T(8,128)S(1)} %get-tuple-element.20.acc, f32[2,4,512,128]{3,2,1,0:T(8,128)S(1)} %get-tuple-element.18.ext.ext_old, f32[1024,128]{1,0:T(8,128)S(1)} %get-tuple-element.21.pacc, f32[1024,128]{1,0:T(8,128)S(1)} %get-tuple-element.19.probe.flat_old, ...), custom_call_target="tpu_custom_call" | custom-call | tf_op jit(solution)/shard_map/last_update/pallas_call | solution.py:639
  129.8 1.0 deliver.1
Async XLA Ops:
  0.6 22.9 %copy-start = (bf16[4,256,256]{2,1,0:T(8,128)(2,1)S(1)}, bf16[4,256,256]{2,1,0:T(8,128)(2,1)}, u32[]{:S(2)}) copy-start(bf16[4,256,256]{2,1,0:T(8,128)(2,1)} %constant.8.clone.tab) | copy-start | bytes 1572868
  0.6 22.9 %copy-start.1 = (bf16[512,512]{1,0:T(8,128)(2,1)S(1)}, bf16[512,512]{1,0:T(8,128)(2,1)}, u32[]{:S(2)}) copy-start(bf16[512,512]{1,0:T(8,128)(2,1)} %constant.7.clone.rtab) | copy-start | bytes 1572868
  0.7 22.9 %copy-start.2 = (bf16[512,512]{1,0:T(8,128)(2,1)S(1)}, bf16[512,512]{1,0:T(8,128)(2,1)}, u32[]{:S(2)}) copy-start(bf16[512,512]{1,0:T(8,128)(2,1)} %constant.6.clone.ltab) | copy-start | bytes 1572868
  0.7 22.9 %copy-start.5 = (s32[16,2]{0,1:T(2,128)S(1)}, s32[16,2]{0,1:T(2,128)}, u32[]{:S(2)}) copy-start(s32[16,2]{0,1:T(2,128)} %param.12) | copy-start | bytes 388
  23.6 14.8 %copy-start.3 = (f32[2,3,3]{2,0,1:T(2,128)S(1)}, f32[2,3,3]{2,0,1:T(2,128)}, u32[]{:S(2)}) copy-start(f32[2,3,3]{2,0,1:T(2,128)} %param.15) | copy-start | bytes 220
  23.6 14.8 %copy-start.4 = (f32[2,3,3]{2,0,1:T(2,128)S(1)}, f32[2,3,3]{2,0,1:T(2,128)}, u32[]{:S(2)}) copy-start(f32[2,3,3]{2,0,1:T(2,128)} %param.16) | copy-start | bytes 220
